TPU v7x, 128 devices: a whole 4x4x4 slice. The times are simulated.
128 devices in a mesh: member: 8 (over y_lo, x), grid: 16 (over y_hi, z, core).
Axes of the slice: x: 4, y: 4 (y_hi: 2, y_lo: 2; y = y_hi * 2 + y_lo), z: 4, core: 2. Of those that a mesh axis runs over, the one named last changes fastest.
Arguments:
- embedding_tensor: bfloat16 [16, 1024, 16384], P('member', None, 'grid'), may hold values from -6 to 6
- first_projection_matrix: bfloat16 [1024, 1024], replicated, may hold values from -0.1875 to 0.1875
- variable_projection_matrix: bfloat16 [1024, 100], replicated, may hold values from -0.1875 to 0.1875
- target: bfloat16 [100, 16384], P(None, 'grid'), may hold values from -5 to 5
- var_weight: float32 [100], replicated, may hold values from 0.3 to 3
- area_weight: float32 [16384], P('grid'), may hold values from 0.06 to 1.8, as said below
Outputs:
- embedding_derivative: bfloat16 [16, 1024, 16384], P('member', None, 'grid')
- grad_in: float32 [1024, 1024], replicated
- grad_out: float32 [1024, 100], replicated
- crps_penalty: float32 [], replicated
Inputs may be any that keep to these rules, and one draw needn't show every extreme that they name: `area_weight`: area weights are positive.
All inputs are finite; a program needn't handle non-finite values.
Results may differ from a plain program's by a relative error of at most 0.003.
The roundings to bfloat16 on the way count: a program that leaves them out, or rounds other values in their place, can miss the bound.
Values sent between devices are 32-bit elements; how exact they have to be, the bound alone decides.
A program may use at most 128 MiB of HBM per device.

v0:
```python
import math

import jax
import jax.numpy as jnp
from jax import lax
from jax.sharding import PartitionSpec as P

SMOOTH_WIDTH = 0.1
ALPHA_FAIR = 0.95


def magnitude_derivative(values):
    return values * lax.rsqrt(values * values + SMOOTH_WIDTH * SMOOTH_WIDTH)


def softened_magnitude(values):
    return jnp.sqrt(values * values + SMOOTH_WIDTH * SMOOTH_WIDTH) - SMOOTH_WIDTH


def per_device(
    embedding_tensor,
    first_projection_matrix,
    variable_projection_matrix,
    target,
    var_weight,
    area_weight,
):
    local_members = embedding_tensor.shape[0]
    local_cells = embedding_tensor.shape[2]
    member_count = lax.axis_size("member")
    total_members = local_members * member_count
    location_number = local_cells * lax.axis_size("grid")
    unbiased_blend_factor = (1.0 - (1.0 - ALPHA_FAIR) / total_members) / (total_members - 1)
    area_total = lax.psum(jnp.sum(area_weight), "grid")
    mean_area = area_total / location_number
    variable_normaliser = (area_weight / mean_area)[None, :] * var_weight[:, None]
    verifying_truth = target.astype(jnp.float32)
    intermediate_linear_sum = jnp.einsum(
        "hi,mhc->mic", first_projection_matrix, embedding_tensor, preferred_element_type=jnp.float32
    )
    intermediate_response = jax.nn.gelu(intermediate_linear_sum).astype(jnp.bfloat16)
    lone_estimate = jnp.einsum(
        "zq,bzu->bqu",
        variable_projection_matrix,
        intermediate_response,
        preferred_element_type=jnp.float32,
    )
    pairwise_ensemble_gaps = (
        lone_estimate[:, None] - lax.all_gather(lone_estimate, "member", axis=0, tiled=True)[None]
    )
    accumulated_derivative = jnp.sum(magnitude_derivative(pairwise_ensemble_gaps), 1)
    spread_sum = jnp.sum(softened_magnitude(pairwise_ensemble_gaps), (0, 1))
    truth_residual = jnp.sum(softened_magnitude(lone_estimate - verifying_truth[None]), 0)
    estimate_derivative = (
        variable_normaliser[None]
        * (
            magnitude_derivative(lone_estimate - verifying_truth[None])
            - unbiased_blend_factor * accumulated_derivative
        )
    ).astype(jnp.bfloat16)
    loss_part = jnp.sum(
        variable_normaliser
        * (
            truth_residual / total_members
            - unbiased_blend_factor / (2 * total_members) * spread_sum
        )
    )
    grad_second = jnp.einsum(
        "mhc,mvc->hv",
        intermediate_response,
        estimate_derivative,
        preferred_element_type=jnp.float32,
    )
    grad_act = jnp.einsum(
        "hv,mvc->mhc",
        variable_projection_matrix,
        estimate_derivative,
        preferred_element_type=jnp.float32,
    )
    unused_out, backward = jax.vjp(jax.nn.gelu, intermediate_linear_sum)
    grad_pre = backward(grad_act)[0].astype(jnp.bfloat16)
    embedding_derivative = jnp.einsum(
        "hi,mic->mhc", first_projection_matrix, grad_pre, preferred_element_type=jnp.float32
    ).astype(jnp.bfloat16)
    grad_first = jnp.einsum(
        "mhc,mic->hi", embedding_tensor, grad_pre, preferred_element_type=jnp.float32
    )
    grad_first, grad_second, accumulated_penalty = lax.psum(
        (grad_first, grad_second, loss_part), ("member", "grid")
    )
    rescale = 1.0 / math.sqrt(total_members * location_number)
    crps_penalty = accumulated_penalty / (location_number * lone_estimate.shape[1])
    return (embedding_derivative, grad_first * rescale, grad_second * rescale, crps_penalty)


def solution(mesh):
    in_specs = (P("member", None, "grid"), P(), P(), P(None, "grid"), P(), P("grid"))
    out_specs = (P("member", None, "grid"), P(), P(), P())
    return jax.shard_map(
        per_device, mesh=mesh, in_specs=in_specs, out_specs=out_specs, check_vma=False
    )
```

profile of v0, /device:TPU:1, one launch (start us, length us, event | category | flops | bytes accessed | tf_op | source)
XLA Modules:
  0.0 334.1 jit_solution(13695051325408276331)
XLA Ops:
  7.2 0.0 copy-start
  7.2 0.0 copy-start.8
  7.2 0.0 all-gather.2.cloned.1.call-start
  7.3 1.5 copy-done
  8.8 10.9 %fusion.16 = (bf16[2,1024,1024]{1,2,0:T(8,128)(2,1)S(1)}, f32[2,1024,1024]{2,1,0:T(8,128)}) fusion(bf16[2,1024,1024]{2,1,0:T(8,128)(2,1)} %param.6, bf16[1024,1024]{1,0:T(8,128)(2,1)S(1)} %copy-done), kind=kOutput, calls=%fused_computation.23 | convolution fusion | flops 4313841664 | bytes 18874368 | tf_op jit(solution)/shard_map/hi,mhc->mic/dot_general | solution.py:38
  19.7 2.0 copy-done.1
  21.7 2.3 convolution_bitcast_fusion.1
  24.1 0.0 all-gather.2.cloned.1.call-update
  24.1 0.0 all-reduce.3.cloned.1.call-start
  24.1 0.6 reduce_sum.45
  24.7 86.9 %psum.28 = f32[]{:T(128)} all-reduce(f32[]{:T(128)} %reduce_sum.45), channel_id=1, replica_groups=mesh['member'=8,'grid'=16] {'grid'}, use_global_device_ids=true, to_apply=%region_1.0 | all-reduce | flops 1 | bytes 8 | tf_op jit(solution)/shard_map/psum | solution.py:34
  111.7 1.0 convert_element_type.19
  113.3 0.9 broadcast_multiply_fusion.2
  114.2 6.9 %copy.24 = f32[16,100,1024]{2,0,1:T(8,128)S(1)} copy(f32[16,100,1024]{2,1,0:T(8,128)} %all-gather.2.cloned.1.call-done) | data formatting | bytes 13107200 | tf_op jit(solution)/shard_map/all_gather | solution.py:49
  121.1 0.0 copy-start.9
  121.1 18.3 %fusion.4 = (f32[100,1024]{1,0:T(8,128)}, f32[2,100,1024]{2,1,0:T(8,128)S(1)}) fusion(f32[16,100,1024]{2,0,1:T(8,128)S(1)} %copy.24, f32[2,100,1024]{2,1,0:T(8,128)S(1)} %copy-done.3), kind=kLoop, calls=%fused_computation.6 | loop fusion | flops 22630400 | bytes 8601600 | tf_op jit(solution)/shard_map/reduce_sum | solution.py:52
  139.5 1.3 add_reduce_fusion
  140.7 1.5 convolution_bitcast_fusion.2
  142.3 0.0 copy-start.12
  142.3 6.6 %fusion.12 = bf16[2,1024,1024]{1,2,0:T(8,128)(2,1)S(1)} fusion(f32[2,1024,1024]{2,1,0:T(8,128)S(1)} %bitcast.57, bf16[2,100,1024]{2,1,0:T(8,128)(2,1)S(1)} %get-tuple-element.21, bf16[1024,100]{0,1:T(8,128)(2,1)S(1)} %copy-done.9), kind=kOutput, calls=%fused_computation.16 | convolution fusion | flops 461373440 | bytes 13197312 | tf_op jit(solution)/shard_map/hv,mvc->mhc/dot_general | solution.py:74
  148.8 0.0 copy-start.13
  148.8 2.0 copy-done.13
  150.8 6.1 %convolution_bitcast_fusion = f32[1024,1024]{0,1:T(8,128)} fusion(bf16[2,1024,1024]{1,2,0:T(8,128)(2,1)S(1)} %fusion.12, bf16[2,1024,1024]{2,1,0:T(8,128)(2,1)S(1)} %copy-done.12), kind=kOutput, calls=%fused_computation.25 | convolution fusion | flops 4294967296 | bytes 12582912 | tf_op jit(solution)/shard_map/mhc,mic->hi/dot_general | solution.py:85
  157.0 0.0 all-reduce.3.cloned.1.call-update
  157.0 0.8 multiply_reduce_fusion
  157.8 69.5 %psum.31 = f32[]{:T(128)} all-reduce(f32[]{:T(128)} %multiply_reduce_fusion), channel_id=1, replica_groups=mesh['member'=8,'grid'=16] {'member','grid'}, use_global_device_ids=true, to_apply=%region_8.0 | all-reduce | flops 1 | bytes 8 | tf_op jit(solution)/shard_map/psum | solution.py:88
  227.3 8.3 %convert_bitcast_fusion = bf16[2,1024,1024]{1,2,0:T(8,128)(2,1)} fusion(bf16[2,1024,1024]{1,2,0:T(8,128)(2,1)} %copy-done.13, bf16[1024,1024]{1,0:T(8,128)(2,1)S(1)} %copy-done), kind=kOutput, calls=%fused_computation.24 | convolution fusion | flops 4297064448 | bytes 10485760 | tf_op jit(solution)/shard_map/hi,mic->mhc/dot_general | solution.py:82
  235.7 6.2 %copy.27 = bf16[2,1024,1024]{2,1,0:T(8,128)(2,1)} copy(bf16[2,1024,1024]{1,2,0:T(8,128)(2,1)} %convert_bitcast_fusion) | data formatting | bytes 8388608
  242.5 72.4 %all-reduce.3.cloned.1.call-done = (f32[1024,1024]{0,1:T(8,128)}, f32[1024,100]{0,1:T(8,128)}) async-done(((f32[1024,1024]{0,1:T(8,128)}, f32[1024,100]{0,1:T(8,128)}), (f32[1024,1024]{0,1:T(8,128)}, f32[1024,100]{0,1:T(8,128)})) %all-reduce.3.cloned.1.call-update) | async-done | bytes 4603920 | tf_op jit(solution)/shard_map/psum | solution.py:88
  315.0 5.1 %broadcast_multiply_fusion = f32[1024,1024]{0,1:T(8,128)} fusion(f32[1024,1024]{0,1:T(8,128)} %get-tuple-element.18), kind=kLoop, calls=%fused_computation.29 | loop fusion | flops 1048576 | bytes 8388608 | tf_op jit(solution)/shard_map/mul | solution.py:93
  320.0 5.3 %copy.28 = f32[1024,1024]{1,0:T(8,128)} copy(f32[1024,1024]{0,1:T(8,128)} %broadcast_multiply_fusion) | data formatting | bytes 8388608
  325.4 0.8 broadcast_multiply_fusion.1
  (27 shorter events, 0.1 us)
Async XLA Ops:
  7.2 1.6 copy-start
  7.2 14.5 %copy-start.8 = (bf16[1024,100]{0,1:T(8,128)(2,1)S(1)}, bf16[1024,100]{0,1:T(8,128)(2,1)}, u32[]{:S(2)}) copy-start(bf16[1024,100]{0,1:T(8,128)(2,1)} %param.8) | copy-start | bytes 614404
  7.2 16.9 %copy-start.10 = (f32[1024]{0:T(1024)S(1)}, f32[1024]{0:T(1024)}, u32[]{:S(2)}) copy-start(f32[1024]{0:T(1024)} %param.11) | copy-start | bytes 12292
  7.2 106.1 %copy-start.11 = (f32[100]{0:T(128)S(1)}, f32[100]{0:T(128)}, u32[]{:S(2)}) copy-start(f32[100]{0:T(128)} %param.10) | copy-start | bytes 1204
  7.2 107.0 %all-gather.2.cloned.1.call-start = ((), (), s32[]{:S(2)}) async-start(), calls=%async_computation | async-start | bytes 7667712 | tf_op jit(solution)/shard_map/all_gather | solution.py:49
  19.7 2.0 copy-start.1
  24.1 97.0 %copy-start.3 = (f32[2,100,1024]{2,1,0:T(8,128)S(1)}, f32[2,100,1024]{2,1,0:T(8,128)}, u32[]{:S(2)}) copy-start(f32[2,100,1024]{2,1,0:T(8,128)} %convolution_bitcast_fusion.1) | copy-start | bytes 2457604
  24.1 290.9 %all-reduce.3.cloned.1.call-start = ((), (), s32[]{:S(2)}) async-start(), calls=%async_computation.1 | async-start | bytes 9240576 | tf_op jit(solution)/shard_map/psum | solution.py:88
  114.2 28.0 %slice-start = ((s8[8388608]{0:T(1024)(128)(4,1)}), s8[4194304]{0:T(1024)(128)(4,1)S(1)}, s32[]{:S(2)}) async-start(s8[8388608]{0:T(1024)(128)(4,1)} %bitcast.56), calls=%async_computation.2 | async-start | bytes 8388608
  121.1 18.4 %copy-start.5 = (f32[100,1024]{1,0:T(8,128)S(1)}, f32[100,1024]{1,0:T(8,128)}, u32[]{:S(2)}) copy-start(f32[100,1024]{1,0:T(8,128)} %broadcast_multiply_fusion.2) | copy-start | bytes 1228804
  121.1 19.6 %copy-start.2 = (bf16[2,1024,1024]{1,2,0:T(8,128)(2,1)S(1)}, bf16[2,1024,1024]{1,2,0:T(8,128)(2,1)}, u32[]{:S(2)}) copy-start(bf16[2,1024,1024]{1,2,0:T(8,128)(2,1)} %copy-done.1) | copy-start | bytes 12582916
  121.1 21.1 %copy-start.9 = (bf16[1024,100]{0,1:T(8,128)(2,1)S(1)}, bf16[1024,100]{0,1:T(8,128)(2,1)}, u32[]{:S(2)}) copy-start(bf16[1024,100]{0,1:T(8,128)(2,1)} %param.8) | copy-start | bytes 614404
  121.1 21.1 %slice-start.1 = ((s8[8388608]{0:T(1024)(128)(4,1)}), s8[4194304]{0:T(1024)(128)(4,1)S(1)}, s32[]{:S(2)}) async-start(s8[8388608]{0:T(1024)(128)(4,1)} %bitcast.56), calls=%async_computation.3 | async-start | bytes 8388608
  142.3 8.6 %copy-start.12 = (bf16[2,1024,1024]{2,1,0:T(8,128)(2,1)S(1)}, bf16[2,1024,1024]{2,1,0:T(8,128)(2,1)}, u32[]{:S(2)}) copy-start(bf16[2,1024,1024]{2,1,0:T(8,128)(2,1)} %param.6) | copy-start | bytes 12582916
  148.8 2.0 copy-start.13
  150.8 6.2 %copy-start.4 = (f32[100,1024]{1,0:T(8,128)S(1)}, f32[100,1024]{1,0:T(8,128)}, u32[]{:S(2)}) copy-start(f32[100,1024]{1,0:T(8,128)} %get-tuple-element.20) | copy-start | bytes 1228804
  150.8 6.2 %copy-start.7 = (f32[100,1024]{1,0:T(8,128)S(1)}, f32[100,1024]{1,0:T(8,128)}, u32[]{:S(2)}) copy-start(f32[100,1024]{1,0:T(8,128)} %get-tuple-element.16) | copy-start | bytes 1228804
  315.0 10.4 %copy-start.6 = (f32[1024,100]{0,1:T(8,128)S(1)}, f32[1024,100]{0,1:T(8,128)}, u32[]{:S(2)}) copy-start(f32[1024,100]{0,1:T(8,128)} %get-tuple-element.19) | copy-start | bytes 1228804
Sparse Core Ops, SparseCore 0:
  24.2 80.3 all-gather.1
  157.1 157.7 all-reduce.2
where the time goes:
time: 335 us; the launch traced here: 334 us
  blocking collectives  156 us (47%)
  waiting for transfers between devices  72.5 us (22%)
  matrix products  35.8 us (11%)
  other arithmetic  28.7 us (9%)
  local copies, waits for them, and re-layouts  24 us (7%)
  between operations  16.6 us (5%)
    psum x1, blocking collectives, per_device(): area_total = lax.psum(jnp.sum(area_weight), 'grid')  86.9 us
    psum x1, waiting for transfers between devices, per_device(): lax.psum((grad_first, grad_second, loss_part), ('member', 'grid'))  72.4 us
    psum x1, blocking collectives, per_device(): lax.psum((grad_first, grad_second, loss_part), ('member', 'grid'))  69.5 us
    reduce_sum x1, other arithmetic, per_device(): spread_sum = jnp.sum(softened_magnitude(pairwise_ensemble_gaps), (0, 1))  18.3 us
    unnamed x34, local copies, waits for them, and re-layouts  17.1 us
    dot_general x1, matrix products, per_device(): jnp.einsum('hi,mhc->mic', first_projection_matrix, embedding_tensor, pref...  10.9 us
    dot_general x1, matrix products, per_device(): jnp.einsum('hi,mic->mhc', first_projection_matrix, grad_pre, preferred_el...  8.33 us
    all_gather x1, local copies, waits for them, and re-layouts, per_device(): lax.all_gather(lone_estimate, 'member', axis=0, tiled=True)[None]  6.88 us
  transfers between devices with their start and end apart: 2, of which 1 were waited for; matrix products, arithmetic and copies ran while one was open for 5% of the time, Pallas kernels for 0%

commit v1 on v0

v1 whole, which is shorter than its diff:
```python
import functools
import math

import jax
import jax.numpy as jnp
from jax import lax
from jax.experimental import pallas as pl
from jax.experimental.pallas import tpu as pltpu
from jax.sharding import PartitionSpec as P

SMOOTH_WIDTH = 0.1
ALPHA_FAIR = 0.95
MESH = pl.DeviceIdType.MESH
F32 = jnp.float32
BF16 = jnp.bfloat16
GELU_A = math.sqrt(2.0 / math.pi)
GELU_B = 0.044715

H = 1024
V = 100
VH = V // 2
VP = 128
CELLS = 1024
MEM = 2
TOTAL_MEM = 16
TOTAL_CELLS = 16384
NQ = 2
CQ = CELLS // NQ
HALF = H // 2
WIDE = H + VP
PW = WIDE // 3
LOSS_COL = 60
ORDERS = (("x", "y", "z"), ("y", "z", "x"), ("z", "x", "y"))
OFFSETS = (2, 1, 3)


def dot(a, b):
    return lax.dot_general(a, b, (((1,), (0,)), ((), ())), preferred_element_type=F32)


def dot_t(a, b):
    return lax.dot_general(a, b, (((1,), (1,)), ((), ())), preferred_element_type=F32)


def gelu_and_derivative(x):
    x2 = x * x
    t = jnp.tanh(x * (GELU_A + (GELU_A * GELU_B) * x2))
    h = 0.5 + 0.5 * t
    y = x * h
    return y, h + (y * (1.0 - t)) * (GELU_A + (3.0 * GELU_A * GELU_B) * x2)


def ds(start, size, multiple):
    return pl.ds(pl.multiple_of(start, multiple), size)


def kernel(
    emb, w1_hbm, w2, target, vw, aw,
    ed_out, wide_out,
    e, w1, w1t, w2p, w2t, act, dg, gv, gp, tgt, vcol, av,
    fs, fr, gs, gr, grad, core_in, s1, r1, s2, r2, s3, full, loss,
    in_sem, area_s, area_r, fs_s, fs_r, gs_s, gs_r, core_s, core_r,
    rs_s, rs_r, ag_s, ag_r, cg_s, cg_r, out_sem,
):
    me = lax.axis_index("member")
    g = lax.axis_index("grid")
    pos = {"x": me % 4, "y": (g // 8) * 2 + me // 4, "z": (g // 2) % 4, "c": g % 2}
    core = pos["c"]

    def device(p):
        return ((p["y"] % 2) * 4 + p["x"], ((p["y"] // 2) * 4 + p["z"]) * 2 + p["c"])

    def moved(**by):
        return {k: (v + by[k]) % (2 if k == "c" else 4) if k in by else v for k, v in pos.items()}

    def member_peer(o):
        return (me // 4 + o // 4) % 2 * 4 + (me % 4 + o % 4) % 4

    def member_from(o):
        return (me // 4 + o // 4) % 2 * 4 + (me % 4 + 4 - o % 4) % 4

    w1_copy = pltpu.make_async_copy(w1_hbm, w1, in_sem.at[4])
    w1_copy.start()

    def emb_copy(q, m):
        sl = pl.ds(q * CQ, CQ)
        return pltpu.make_async_copy(emb.at[m, :, sl], e.at[m, :, sl], in_sem.at[q * 2 + m])

    for q in range(NQ):
        for m in range(MEM):
            emb_copy(q, m).start()

    barrier = pltpu.get_barrier_semaphore()
    for o in range(1, 8):
        pl.semaphore_signal(barrier, inc=1, device_id=(member_peer(o), g), device_id_type=MESH)
    for o in range(1, 16):
        pl.semaphore_signal(barrier, inc=1, device_id=(me, (g + o) % 16), device_id_type=MESH)
    pl.semaphore_signal(
        barrier, inc=1, device_id=((me + 4) % 8, (g + 8) % 16), device_id_type=MESH
    )

    w2p[...] = jnp.zeros_like(w2p)
    w2p[:, 0:VH] = w2[:, 0:VH]
    w2p[:, 64 : 64 + VH] = w2[:, VH:V]
    w2t[...] = w2p[...].T
    t32 = target[...].astype(F32)
    tgt[0] = t32[0:VH]
    tgt[1] = t32[VH:V]
    columns = jnp.broadcast_to(vw[...], (VP, VP)).T
    vcol[0] = columns[0:VH]
    vcol[1] = columns[VH:V]
    av[g] = aw[...]
    loss[...] = jnp.zeros_like(loss)
    w1_copy.wait()
    w1t[...] = w1[...].T

    pl.semaphore_wait(barrier, 23)
    area_copies = []
    for o in range(1, 16):
        copy = pltpu.make_async_remote_copy(
            src_ref=av.at[g], dst_ref=av.at[g], send_sem=area_s.at[o], recv_sem=area_r.at[o],
            device_id=(me, (g + o) % 16), device_id_type=MESH,
        )
        copy.start()
        area_copies.append(copy)

    def exchange(q, o, src, dst, ss, rs):
        return pltpu.make_async_remote_copy(
            src_ref=src.at[q, member_peer(o)], dst_ref=dst.at[q, me],
            send_sem=ss.at[q, o], recv_sem=rs.at[q, o],
            device_id=(member_peer(o), g), device_id_type=MESH,
        )

    def exchange_in(q, o, src, dst, ss, rs):
        return pltpu.make_async_remote_copy(
            src_ref=src.at[q, member_peer(o)], dst_ref=dst.at[q, member_from(o)],
            send_sem=ss.at[q, o], recv_sem=rs.at[q, o],
            device_id=(member_peer(o), g), device_id_type=MESH,
        )

    PEERS = (6, 2, 5, 7, 4, 1, 3)

    def send_all(q, src, dst, ss, rs):
        for o in PEERS:
            exchange(q, o, src, dst, ss, rs).start()
        dst[q, me] = src[q, me]

    def receive_all(q, src, dst, ss, rs):
        for o in PEERS:
            exchange_in(q, o, src, dst, ss, rs).wait_recv()

    def forward(q):
        sl = pl.ds(q * CQ, CQ)

        @pl.loop(0, MEM)
        def _(m):
            emb_copy(q, m).wait()
            y, d = gelu_and_derivative(dot(w1t[...], e[m, :, sl]))
            act[m, :, sl] = y.astype(BF16)
            dg[m, :, sl] = d
            fc = dot(w2t[...], act[m, :, sl])
            for r in range(2):
                for l in range(4):
                    fs[q, r * 4 + l, m] = fc[64 * r : 64 * r + VH, 128 * l : 128 * l + 128]

        send_all(q, fs, fr, fs_s, fs_r)

    coef = (1.0 - (1.0 - ALPHA_FAIR) / TOTAL_MEM) / (TOTAL_MEM - 1)
    d2 = SMOOTH_WIDTH * SMOOTH_WIDTH

    def pairwise(q):
        mine_r, mine_l = me // 4, me % 4
        lanes = ds(q * CQ + mine_l * 128, 128, 128)
        mean = jnp.sum(jnp.sum(av[...], axis=0), keepdims=True) / TOTAL_CELLS
        area = aw[pl.ds(q * 4 + mine_l, 1), :] / mean

        def tile(rows, n):
            scale = area * vcol[mine_r, rows, :]
            t = tgt[mine_r, rows, lanes]
            f = [fr[q, k // 2, k % 2, rows, :] for k in range(TOTAL_MEM)]
            s = [None] * TOTAL_MEM
            spread = None
            for i in range(TOTAL_MEM):
                for k in range(i + 1, TOTAL_MEM):
                    d = f[i] - f[k]
                    w = d * d + d2
                    inv = lax.rsqrt(w)
                    slope = d * inv
                    s[i] = slope if s[i] is None else s[i] + slope
                    s[k] = -slope if s[k] is None else s[k] - slope
                    smooth = w * inv - SMOOTH_WIDTH
                    spread = smooth if spread is None else spread + smooth
            truth = None
            for i in range(TOTAL_MEM):
                d = f[i] - t
                w = d * d + d2
                inv = lax.rsqrt(w)
                gs[q, i // 2, i % 2, rows, :] = scale * (d * inv - coef * s[i])
                smooth = w * inv - SMOOTH_WIDTH
                truth = smooth if truth is None else truth + smooth
            loss[0:n, :] += scale * (truth / TOTAL_MEM - (coef / TOTAL_MEM) * spread)

        @pl.loop(0, VH // 8)
        def _(i):
            tile(ds(i * 8, 8, 8), 8)

        tile(pl.ds(VH // 8 * 8, VH % 8), VH % 8)
        send_all(q, gs, gr, gs_s, gs_r)

    def backward(q):
        sl = pl.ds(q * CQ, CQ)
        zeros = jnp.zeros((64 - VH, 128), F32)

        @pl.loop(0, MEM)
        def _(m):
            for r in range(2):
                for l in range(4):
                    block = jnp.concatenate([gr[q, r * 4 + l, m], zeros], axis=0)
                    gv[m, 64 * r : 64 * r + 64, q * CQ + 128 * l : q * CQ + 128 * l + 128] = (
                        block.astype(BF16)
                    )
            gp[m, :, sl] = (dot(w2p[...], gv[m, :, sl]) * dg[m, :, sl]).astype(BF16)

    def weight_gradients(q, half):
        sl = pl.ds(q * CQ, CQ)
        rows = ds(half * HALF, HALF, HALF)

        @pl.loop(0, 4)
        def _(j):
            cols = ds(j * 256, 256, 256)
            new = dot_t(e[0, rows, sl], gp[0, cols, sl]) + dot_t(e[1, rows, sl], gp[1, cols, sl])
            if q == 0:
                grad[rows, cols] = new
            else:
                grad[rows, cols] += new

        new = dot_t(act[0, rows, sl], gv[0, :, sl]) + dot_t(act[1, rows, sl], gv[1, :, sl])
        if q == 0:
            grad[rows, H:WIDE] = new
        else:
            grad[rows, H:WIDE] += new

    def embedding_derivative(m, q):
        sl = pl.ds(q * CQ, CQ)
        e[m, :, sl] = dot(w1[...], gp[m, :, sl]).astype(BF16)
        copy = pltpu.make_async_copy(e.at[m, :, sl], ed_out.at[m, :, sl], out_sem.at[q * 2 + m])
        copy.start()
        return copy

    def part_cols(p):
        return pl.ds(p * PW, PW)

    forward(0)
    forward(1)
    for copy in area_copies:
        copy.wait()
    receive_all(0, fs, fr, fs_s, fs_r)
    pairwise(0)
    receive_all(1, fs, fr, fs_s, fs_r)
    pairwise(1)
    receive_all(0, gs, gr, gs_s, gs_r)
    backward(0)
    weight_gradients(0, 0)
    weight_gradients(0, 1)
    receive_all(1, gs, gr, gs_s, gs_r)
    backward(1)
    weight_gradients(1, 1 - core)
    own_loss = jnp.sum(loss[...], keepdims=True)
    row = lax.broadcasted_iota(jnp.int32, (8, VP), 0)
    col = lax.broadcasted_iota(jnp.int32, (8, VP), 1)
    grad[0:8, H:WIDE] += jnp.where((row == 0) & (col == LOSS_COL), own_loss, 0.0)

    def core_copy(s, p, half):
        k = (pos[ORDERS[p][0]] + s) % 4
        return pltpu.make_async_remote_copy(
            src_ref=grad.at[ds(half * HALF + k * 128, 128, 128), part_cols(p)],
            dst_ref=core_in.at[ds(k * 128, 128, 128), part_cols(p)],
            send_sem=core_s.at[s, p], recv_sem=core_r.at[s, p],
            device_id=device(moved(c=1)), device_id_type=MESH,
        )

    steps = OFFSETS + (0,)
    for s in steps:
        for p in range(3):
            core_copy(s, p, 1 - core).start()
    weight_gradients(1, core)

    def block_rows(p, ks):
        start = core * HALF
        for k, size in zip(ks, (128, 32, 8)):
            start = start + k * size
        return start

    def rs1(s, p):
        axis = ORDERS[p][0]
        k = (pos[axis] + s) % 4
        return pltpu.make_async_remote_copy(
            src_ref=grad.at[ds(block_rows(p, [k]), 128, 128), part_cols(p)],
            dst_ref=s1.at[p, s - 1], send_sem=rs_s.at[0, p, s], recv_sem=rs_r.at[0, p, s],
            device_id=device(moved(**{axis: s})), device_id_type=MESH,
        )

    ed_copies = []
    tiles = [(0, 0), (1, 0), (0, 1), (1, 1)]
    for n, s in enumerate(steps):
        for p in range(3):
            core_copy(s, p, 1 - core).wait_recv()
            k = (pos[ORDERS[p][0]] + s) % 4
            rows = ds(block_rows(p, [k]), 128, 128)
            cols = part_cols(p)
            grad[rows, cols] += core_in[ds(k * 128, 128, 128), cols]
            if s:
                rs1(s, p).start()
        ed_copies.append(embedding_derivative(*tiles[n]))

    for p in range(3):
        for s in OFFSETS:
            rs1(s, p).wait_recv()
        k = pos[ORDERS[p][0]]
        rows = ds(block_rows(p, [k]), 128, 128)
        r1[p] = grad[rows, part_cols(p)] + s1[p, 0] + s1[p, 1] + s1[p, 2]

    def rs2(s, p):
        axis = ORDERS[p][1]
        k = (pos[axis] + s) % 4
        return pltpu.make_async_remote_copy(
            src_ref=r1.at[p, ds(k * 32, 32, 32)], dst_ref=s2.at[p, s - 1],
            send_sem=rs_s.at[1, p, s], recv_sem=rs_r.at[1, p, s],
            device_id=device(moved(**{axis: s})), device_id_type=MESH,
        )

    def rs3(s, p):
        axis = ORDERS[p][2]
        k = (pos[axis] + s) % 4
        return pltpu.make_async_remote_copy(
            src_ref=r2.at[p, ds(k * 8, 8, 8)], dst_ref=s3.at[p, s - 1],
            send_sem=rs_s.at[2, p, s], recv_sem=rs_r.at[2, p, s],
            device_id=device(moved(**{axis: s})), device_id_type=MESH,
        )

    for p in range(3):
        for s in OFFSETS:
            rs2(s, p).start()
    for p in range(3):
        for s in OFFSETS:
            rs2(s, p).wait_recv()
        k = pos[ORDERS[p][1]]
        r2[p] = r1[p, ds(k * 32, 32, 32)] + s2[p, 0] + s2[p, 1] + s2[p, 2]
        for s in OFFSETS:
            rs3(s, p).start()

    def gather_copy(level, p, s, arriving):
        axis = ORDERS[p][level]
        ks = [pos[a] for a in ORDERS[p][: level + 1]]
        if arriving:
            ks[level] = (ks[level] + 4 - s) % 4
        size = (128, 32, 8)[level]
        at = full.at[ds(block_rows(p, ks), size, size), part_cols(p)]
        return pltpu.make_async_remote_copy(
            src_ref=at, dst_ref=at, send_sem=ag_s.at[level, p, s], recv_sem=ag_r.at[level, p, s],
            device_id=device(moved(**{axis: s})), device_id_type=MESH,
        )

    rescale = 1.0 / math.sqrt(TOTAL_MEM * TOTAL_CELLS)
    for p in range(3):
        for s in OFFSETS:
            rs3(s, p).wait_recv()
        ks = [pos[a] for a in ORDERS[p]]
        total = r2[p, ds(ks[2] * 8, 8, 8)] + s3[p, 0] + s3[p, 1] + s3[p, 2]
        full[ds(block_rows(p, ks), 8, 8), part_cols(p)] = total * rescale
        for s in OFFSETS:
            gather_copy(2, p, s, False).start()

    for level in (2, 1):
        for p in range(3):
            for s in OFFSETS:
                gather_copy(level, p, s, True).wait_recv()
            for s in OFFSETS:
                gather_copy(level - 1, p, s, False).start()

    def block(p, s, c):
        k = (pos[ORDERS[p][0]] + 4 - s) % 4
        return (ds(c * HALF + k * 128, 128, 128), part_cols(p))

    def core_gather(p, s, c):
        at = full.at[block(p, s, c)]
        return pltpu.make_async_remote_copy(
            src_ref=at, dst_ref=at, send_sem=cg_s.at[p, s], recv_sem=cg_r.at[p, s],
            device_id=device(moved(c=1)), device_id_type=MESH,
        )

    out_copies = []

    def store(p, s, c, n):
        where = block(p, s, c)
        copy = pltpu.make_async_copy(full.at[where], wide_out.at[where], out_sem.at[4 + n])
        copy.start()
        out_copies.append(copy)

    for p in range(3):
        core_gather(p, 0, core).start()
        store(p, 0, core, p)
    for s in (1, 3, 2):
        for p in range(3):
            gather_copy(0, p, s, True).wait_recv()
            core_gather(p, s, core).start()
            store(p, s, core, s * 3 + p)
    for s in (0, 1, 3, 2):
        for p in range(3):
            core_gather(p, s, 1 - core).wait_recv()
            store(p, s, 1 - core, 12 + s * 3 + p)

    for q in range(NQ):
        for o in PEERS:
            exchange(q, o, fs, fr, fs_s, fs_r).wait_send()
            exchange(q, o, gs, gr, gs_s, gs_r).wait_send()
    for p in range(3):
        for s in steps:
            core_copy(s, p, 1 - core).wait_send()
            core_gather(p, s, core).wait_send()
        for s in OFFSETS:
            rs1(s, p).wait_send()
            rs2(s, p).wait_send()
            rs3(s, p).wait_send()
            for level in range(3):
                gather_copy(level, p, s, False).wait_send()
    for copy in ed_copies + out_copies:
        copy.wait()


def per_device(
    embedding_tensor,
    first_projection_matrix,
    variable_projection_matrix,
    target,
    var_weight,
    area_weight,
):
    vmem = pl.BlockSpec(memory_space=pltpu.VMEM)
    hbm = pl.BlockSpec(memory_space=pl.ANY)
    dma = pltpu.SemaphoreType.DMA
    big = (MEM, H, CELLS)
    swap = (NQ, 8, MEM, VH, 128)
    ed, wide = pl.pallas_call(
        kernel,
        name="decoder_crps",
        out_shape=(
            jax.ShapeDtypeStruct(big, BF16),
            jax.ShapeDtypeStruct((H, WIDE), F32),
        ),
        in_specs=[hbm, hbm, vmem, vmem, vmem, vmem],
        out_specs=(hbm, hbm),
        scratch_shapes=[
            pltpu.VMEM(big, BF16),
            pltpu.VMEM((H, H), BF16),
            pltpu.VMEM((H, H), BF16),
            pltpu.VMEM((H, VP), BF16),
            pltpu.VMEM((VP, H), BF16),
            pltpu.VMEM(big, BF16),
            pltpu.VMEM(big, F32),
            pltpu.VMEM((MEM, VP, CELLS), BF16),
            pltpu.VMEM(big, BF16),
            pltpu.VMEM((2, VH, CELLS), F32),
            pltpu.VMEM((2, VH, 128), F32),
            pltpu.VMEM((16, 8, 128), F32),
            pltpu.VMEM(swap, F32),
            pltpu.VMEM(swap, F32),
            pltpu.VMEM(swap, F32),
            pltpu.VMEM(swap, F32),
            pltpu.VMEM((H, WIDE), F32),
            pltpu.VMEM((HALF, WIDE), F32),
            pltpu.VMEM((3, 3, 128, PW), F32),
            pltpu.VMEM((3, 128, PW), F32),
            pltpu.VMEM((3, 3, 32, PW), F32),
            pltpu.VMEM((3, 32, PW), F32),
            pltpu.VMEM((3, 3, 8, PW), F32),
            pltpu.VMEM((H, WIDE), F32),
            pltpu.VMEM((8, 128), F32),
            dma((5,)),
            dma((16,)), dma((16,)),
            dma((NQ, 8)), dma((NQ, 8)),
            dma((NQ, 8)), dma((NQ, 8)),
            dma((4, 3)), dma((4, 3)),
            dma((3, 3, 4)), dma((3, 3, 4)),
            dma((3, 3, 4)), dma((3, 3, 4)),
            dma((3, 4)), dma((3, 4)),
            dma((28,)),
        ],
        compiler_params=pltpu.CompilerParams(
            collective_id=0, has_side_effects=True, vmem_limit_bytes=60 * 2**20
        ),
        cost_estimate=pl.CostEstimate(
            flops=15_000_000_000, bytes_accessed=20_000_000, transcendentals=4_000_000
        ),
    )(
        embedding_tensor,
        first_projection_matrix,
        variable_projection_matrix,
        target,
        jnp.pad(var_weight, (0, VP - V)).reshape(1, VP),
        area_weight.reshape(8, 128),
    )
    grad_out = jnp.concatenate([wide[:, H : H + VH], wide[:, H + 64 : H + 64 + VH]], axis=1)
    rescale = 1.0 / math.sqrt(TOTAL_MEM * TOTAL_CELLS)
    crps = wide[0, H + LOSS_COL] / (rescale * TOTAL_CELLS * V)
    return ed, wide[:, :H], grad_out, crps


def solution(mesh):
    in_specs = (P("member", None, "grid"), P(), P(), P(None, "grid"), P(), P("grid"))
    out_specs = (P("member", None, "grid"), P(), P(), P())
    return jax.shard_map(
        per_device, mesh=mesh, in_specs=in_specs, out_specs=out_specs, check_vma=False
    )
```

time: 335 us -> 101 us (0.30)
  blocking collectives: 156 us -> 0 us
  Pallas kernels: 0 us -> 84.2 us
  waiting for transfers between devices: 72.5 us -> 0 us
  matrix products: 35.8 us -> 0 us
  other arithmetic: 28.7 us -> 0.21 us
  between operations: 16.6 us -> 2.44 us
  local copies, waits for them, and re-layouts: 24 us -> 13.7 us
    psum x2 -> x0, blocking collectives: 156 us -> none  [the longest x1 86.9 us: per_device(): area_total = lax.psum(jnp.sum(area_weight), 'grid')]
    pallas_call x0 -> x1, Pallas kernels: none -> 84.2 us  [per_device(): pl.pallas_call(kernel, name='decoder_crps', out_shape=(jax.ShapeDtypeStru...]
    psum x1 -> x0, waiting for transfers between devices: 72.4 us -> none  [per_device(): lax.psum((grad_first, grad_second, loss_part), ('member', 'grid'))]
    dot_general x6 -> x0, matrix products: 35.8 us -> none  [the longest x1 10.9 us: per_device(): jnp.einsum('hi,mhc->mic', first_projection_matrix, embedding_tensor, pref...]
    reduce_sum x4 -> x0, other arithmetic: 21 us -> none  [the longest x1 18.3 us: per_device(): spread_sum = jnp.sum(softened_magnitude(pairwise_ensemble_gaps), (0, 1))]
    unnamed x34 -> x5, local copies, waits for them, and re-layouts: 17.1 us -> 4.78 us
    slice x0 -> x3, local copies, waits for them, and re-layouts: none -> 7.71 us  [the longest x1 4.94 us: per_device(): return (ed, wide[:, :H], grad_out, crps)]
    all_gather x1 -> x0, local copies, waits for them, and re-layouts: 6.88 us -> none  [per_device(): lax.all_gather(lone_estimate, 'member', axis=0, tiled=True)[None]]
  transfers between devices with their start and end apart: 2 -> 0, of which waited for: 1 -> 0; matrix products, arithmetic and copies ran while one was open for 5% -> 0% of each run, Pallas kernels for 0% -> 0%
where the time goes in v1:
time: 101 us
  Pallas kernels  84.2 us (83%)
  local copies, waits for them, and re-layouts  13.7 us (14%)
  between operations  2.44 us (2%)
    pallas_call x1, Pallas kernels, per_device(): pl.pallas_call(kernel, name='decoder_crps', out_shape=(jax.ShapeDtypeStru...  84.2 us
    slice x1, local copies, waits for them, and re-layouts, per_device(): return (ed, wide[:, :H], grad_out, crps)  4.94 us
    unnamed x5, local copies, waits for them, and re-layouts  4.78 us

profile of v1, /device:TPU:1, one launch (start us, length us, event | category | flops | bytes accessed | tf_op | source)
XLA Modules:
  0.0 100.5 jit_solution(17481632965279660275)
XLA Ops:
  0.6 1.8 %copy.10.w2 = bf16[1024,100]{1,0:T(8,128)(2,1)} copy(bf16[1024,100]{0,1:T(8,128)(2,1)} %param.8) | data formatting | bytes 409600 | tf_op args[2]
  2.4 1.2 %pad_bitcast_fusion.vw = f32[1,128]{1,0:T(1,128)} fusion(f32[100]{0:T(128)} %param.10), kind=kLoop, calls=%fused_computation.1 | loop fusion | bytes 912 | tf_op jit(solution)/shard_map/reshape | solution.py:500
  3.6 84.2 %decoder_crps.1 = (bf16[2,1024,1024]{2,1,0:T(8,128)(2,1)}, f32[1024,1152]{1,0:T(8,128)}) custom-call(bf16[2,1024,1024]{2,1,0:T(8,128)(2,1)} %emb.1, bf16[1024,1024]{1,0:T(8,128)(2,1)} %w1_hbm.1, bf16[1024,100]{1,0:T(8,128)(2,1)} %copy.10.w2, bf16[100,1024]{1,0:T(8,128)(2,1)} %target.1, f32[1,128]{1,0:T(1,128)} %pad_bitcast_fusion.vw, f32[8,128]{1,0:T(8,128)} %bitcast.4), custom_call_target="tpu_custom_call" | custom-call | flops 15000000512 | bytes 20000000 | tf_op jit(solution)/shard_map/decoder_crps/pallas_call | solution.py:444
  87.8 1.5 %fusion = (f32[1024,50]{1,0:T(8,128)S(1)}, f32[1024,50]{1,0:T(8,128)S(1)}) fusion(f32[1024,1152]{1,0:T(8,128)} %get-tuple-element.7), kind=kLoop, calls=%fused_computation.2 | loop fusion | bytes 819200 | tf_op jit(solution)/shard_map/slice | solution.py:503
  89.3 0.2 pad_maximum_fusion
  89.5 1.0 copy.11
  90.5 0.0 copy-start
  90.5 4.9 %slice.12 = f32[1024,1024]{1,0:T(8,128)} slice(f32[1024,1152]{1,0:T(8,128)} %get-tuple-element.7), slice={[0:1024], [0:1024]} | slice | bytes 8388608 | tf_op jit(solution)/shard_map/slice | solution.py:506
  95.4 1.3 %slice.15 = f32[1,1]{1,0:T(1,128)} slice(f32[1024,1152]{1,0:T(8,128)} %get-tuple-element.7), slice={[0:1], [1084:1085]} | slice | bytes 8 | tf_op jit(solution)/shard_map/slice | solution.py:505
  97.4 0.0 copy-done
  97.4 2.0 %copy.13 = bf16[2,1024,1024]{2,1,0:T(8,128)(2,1)} copy(bf16[2,1024,1024]{2,1,0:T(8,128)(2,1)S(1)} %copy-done) | data formatting | bytes 8388608
Async XLA Ops:
  90.5 6.9 %copy-start = (bf16[2,1024,1024]{2,1,0:T(8,128)(2,1)S(1)}, bf16[2,1024,1024]{2,1,0:T(8,128)(2,1)}, u32[]{:S(2)}) copy-start(bf16[2,1024,1024]{2,1,0:T(8,128)(2,1)} %get-tuple-element.18) | copy-start | bytes 12582916

commit v2 on v1

v2 whole, which is shorter than its diff:
```python
import functools
import math

import jax
import jax.numpy as jnp
from jax import lax
from jax.experimental import pallas as pl
from jax.experimental.pallas import tpu as pltpu
from jax.sharding import PartitionSpec as P

SMOOTH_WIDTH = 0.1
ALPHA_FAIR = 0.95
MESH = pl.DeviceIdType.MESH
F32 = jnp.float32
BF16 = jnp.bfloat16
GELU_A = math.sqrt(2.0 / math.pi)
GELU_B = 0.044715

H = 1024
V = 100
VH = V // 2
VP = 128
CELLS = 1024
MEM = 2
TOTAL_MEM = 16
TOTAL_CELLS = 16384
NQ = 2
CQ = CELLS // NQ
HALF = H // 2
WIDE = H + VP
PW = WIDE // 3
LOSS_COL = 60
ORDERS = (("x", "y", "z"), ("y", "z", "x"), ("z", "x", "y"))
OFFSETS = (2, 1, 3)


def dot(a, b):
    return lax.dot_general(a, b, (((1,), (0,)), ((), ())), preferred_element_type=F32)


def dot_t(a, b):
    return lax.dot_general(a, b, (((1,), (1,)), ((), ())), preferred_element_type=F32)


def gelu_and_derivative(x):
    x2 = x * x
    t = jnp.tanh(x * (GELU_A + (GELU_A * GELU_B) * x2))
    h = 0.5 + 0.5 * t
    y = x * h
    return y, h + (y * (1.0 - t)) * (GELU_A + (3.0 * GELU_A * GELU_B) * x2)


def ds(start, size, multiple):
    return pl.ds(pl.multiple_of(start, multiple), size)


def kernel(
    emb, w1_hbm, w2_t, target, vw, aw,
    ed, full,
    e, w1, w1t, w2p, w2t, act, dg, gv, gp, tgt, vcol, av,
    fs, fr, gs, gr, grad, core_in, s1, r1, s2, r2, s3, loss,
    in_sem, area_s, area_r, fs_s, fs_r, gs_s, gs_r, core_s, core_r,
    rs_s, rs_r, ag_s, ag_r, cg_s, cg_r,
):
    me = lax.axis_index("member")
    g = lax.axis_index("grid")
    pos = {"x": me % 4, "y": (g // 8) * 2 + me // 4, "z": (g // 2) % 4, "c": g % 2}
    core = pos["c"]
    sent = {}

    def start(key, copy):
        copy.start()
        sent[key] = copy

    def arrived(key, copy):
        copy.wait_recv()

    def device(p):
        return ((p["y"] % 2) * 4 + p["x"], ((p["y"] // 2) * 4 + p["z"]) * 2 + p["c"])

    def moved(**by):
        return {k: (v + by[k]) % (2 if k == "c" else 4) if k in by else v for k, v in pos.items()}

    def remote(src, dst, send_sem, recv_sem, to):
        return pltpu.make_async_remote_copy(
            src_ref=src, dst_ref=dst, send_sem=send_sem, recv_sem=recv_sem,
            device_id=to, device_id_type=MESH,
        )

    def member_peer(o):
        return (me // 4 + o // 4) % 2 * 4 + (me % 4 + o % 4) % 4

    def member_from(o):
        return (me // 4 + o // 4) % 2 * 4 + (me % 4 + 4 - o % 4) % 4

    def emb_copy(q, m):
        sl = pl.ds(q * CQ, CQ)
        return pltpu.make_async_copy(emb.at[m, :, sl], e.at[m, :, sl], in_sem.at[q * 2 + m])

    def area_copy(o):
        return remote(av.at[g], av.at[g], area_s.at[o], area_r.at[o], (me, (g + o) % 16))

    def area_arrival(o):
        at = av.at[(g + 16 - o) % 16]
        return remote(at, at, area_s.at[o], area_r.at[o], (me, (g + o) % 16))

    def begin():
        w1_copy = pltpu.make_async_copy(w1_hbm, w1, in_sem.at[4])
        w1_copy.start()
        for q in range(NQ):
            for m in range(MEM):
                emb_copy(q, m).start()

        barrier = pltpu.get_barrier_semaphore()
        peers = [(member_peer(o), g) for o in range(1, 8)]
        peers += [(me, (g + o) % 16) for o in range(1, 16)]
        peers += [((me + 4) % 8, (g + 8) % 16)]
        for peer in peers:
            pl.semaphore_signal(barrier, inc=1, device_id=peer, device_id_type=MESH)

        w2t[...] = jnp.zeros_like(w2t)
        wide = w2_t[...].astype(F32)
        gap = jnp.zeros((64 - VH, H), F32)
        w2t[0:64] = jnp.concatenate([wide[0:VH], gap], axis=0).astype(BF16)
        w2t[64:VP] = jnp.concatenate([wide[VH:V], gap], axis=0).astype(BF16)
        w2p[...] = w2t[...].T
        t32 = target[...].astype(F32)
        tgt[0] = t32[0:VH]
        tgt[1] = t32[VH:V]
        columns = jnp.broadcast_to(vw[...], (VP, V)).T
        vcol[0] = columns[0:VH]
        vcol[1] = columns[VH:V]
        av[g] = aw[...]
        loss[...] = jnp.zeros_like(loss)
        w1_copy.wait()
        w1t[...] = w1[...].T

        pl.semaphore_wait(barrier, 23)
        for o in range(1, 16):
            start(("area", o), area_copy(o))

    def exchange(q, o, src, dst, ss, rs, arriving):
        slot = member_from(o) if arriving else me
        return remote(
            src.at[q, member_peer(o)], dst.at[q, slot], ss.at[q, o], rs.at[q, o],
            (member_peer(o), g),
        )

    PEERS = (6, 2, 5, 7, 4, 1, 3)
    FORECAST = (fs, fr, fs_s, fs_r)
    BACK = (gs, gr, gs_s, gs_r)

    def send_all(name, q, way):
        for o in PEERS:
            start((name, q, o), exchange(q, o, *way, False))
        src, dst = way[:2]
        dst[q, me] = src[q, me]

    def receive_all(name, q, way):
        for o in PEERS:
            arrived((name, q, o), exchange(q, o, *way, True))

    def forward(q):
        sl = pl.ds(q * CQ, CQ)

        @pl.loop(0, MEM)
        def _(m):
            emb_copy(q, m).wait()
            y, d = gelu_and_derivative(dot(w1t[...], e[m, :, sl]))
            act[m, :, sl] = y.astype(BF16)
            dg[m, :, sl] = d
            fc = dot(w2t[...], act[m, :, sl])
            for r in range(2):
                for l in range(4):
                    fs[q, r * 4 + l, m] = fc[64 * r : 64 * r + VH, 128 * l : 128 * l + 128]

        send_all("f", q, FORECAST)

    coef = (1.0 - (1.0 - ALPHA_FAIR) / TOTAL_MEM) / (TOTAL_MEM - 1)
    d2 = SMOOTH_WIDTH * SMOOTH_WIDTH

    def pairwise(q):
        mine_r, mine_l = me // 4, me % 4
        lanes = ds(q * CQ + mine_l * 128, 128, 128)
        mean = jnp.sum(jnp.sum(av[...], axis=0), keepdims=True) / TOTAL_CELLS
        area = aw[pl.ds(q * 4 + mine_l, 1), :] / mean

        def tile(rows, n):
            scale = area * vcol[mine_r, rows, :]
            t = tgt[mine_r, rows, lanes]
            f = [fr[q, k // 2, k % 2, rows, :] for k in range(TOTAL_MEM)]
            s = [None] * TOTAL_MEM
            spread = None
            for i in range(TOTAL_MEM):
                for k in range(i + 1, TOTAL_MEM):
                    d = f[i] - f[k]
                    w = d * d + d2
                    inv = lax.rsqrt(w)
                    slope = d * inv
                    s[i] = slope if s[i] is None else s[i] + slope
                    s[k] = -slope if s[k] is None else s[k] - slope
                    smooth = w * inv - SMOOTH_WIDTH
                    spread = smooth if spread is None else spread + smooth
            truth = None
            for i in range(TOTAL_MEM):
                d = f[i] - t
                w = d * d + d2
                inv = lax.rsqrt(w)
                gs[q, i // 2, i % 2, rows, :] = scale * (d * inv - coef * s[i])
                smooth = w * inv - SMOOTH_WIDTH
                truth = smooth if truth is None else truth + smooth
            loss[0:n, :] += scale * (truth / TOTAL_MEM - (coef / TOTAL_MEM) * spread)

        @pl.loop(0, VH // 8)
        def _(i):
            tile(ds(i * 8, 8, 8), 8)

        tile(pl.ds(VH // 8 * 8, VH % 8), VH % 8)
        send_all("g", q, BACK)

    def backward(q):
        sl = pl.ds(q * CQ, CQ)
        zeros = jnp.zeros((64 - VH, 128), F32)

        @pl.loop(0, MEM)
        def _(m):
            for r in range(2):
                for l in range(4):
                    block = jnp.concatenate([gr[q, r * 4 + l, m], zeros], axis=0)
                    gv[m, 64 * r : 64 * r + 64, q * CQ + 128 * l : q * CQ + 128 * l + 128] = (
                        block.astype(BF16)
                    )
            gp[m, :, sl] = (dot(w2p[...], gv[m, :, sl]) * dg[m, :, sl]).astype(BF16)

    def weight_gradients(q, half):
        sl = pl.ds(q * CQ, CQ)
        rows = ds(half * HALF, HALF, HALF)

        @pl.loop(0, 4)
        def _(j):
            cols = ds(j * 256, 256, 256)
            new = dot_t(e[0, rows, sl], gp[0, cols, sl]) + dot_t(e[1, rows, sl], gp[1, cols, sl])
            if q == 0:
                grad[rows, cols] = new
            else:
                grad[rows, cols] += new

        new = dot_t(act[0, rows, sl], gv[0, :, sl]) + dot_t(act[1, rows, sl], gv[1, :, sl])
        if q == 0:
            grad[rows, H:WIDE] = new
        else:
            grad[rows, H:WIDE] += new

    def embedding_derivative(m, q):
        sl = pl.ds(q * CQ, CQ)
        ed[m, :, sl] = dot(w1[...], gp[m, :, sl]).astype(BF16)

    def part_cols(p):
        return pl.ds(p * PW, PW)

    def along(p, level, s):
        return (pos[ORDERS[p][level]] + s) % 4

    def peer(p, level, s):
        return device(moved(**{ORDERS[p][level]: s}))

    def core_copy(s, p):
        k = along(p, 0, s)
        return remote(
            grad.at[ds((1 - core) * HALF + k * 128, 128, 128), part_cols(p)],
            core_in.at[ds(k * 128, 128, 128), part_cols(p)],
            core_s.at[s, p], core_r.at[s, p], device(moved(c=1)),
        )

    def block_rows(ks):
        begin = core * HALF
        for k, size in zip(ks, (128, 32, 8)):
            begin = begin + k * size
        size = (128, 32, 8)[len(ks) - 1]
        return ds(begin, size, size)

    def rs(level, p, s):
        k = along(p, level, s)
        src = (
            grad.at[block_rows([k]), part_cols(p)] if level == 0
            else r1.at[p, ds(k * 32, 32, 32)] if level == 1
            else r2.at[p, ds(k * 8, 8, 8)]
        )
        return remote(
            src, (s1, s2, s3)[level].at[p, s - 1],
            rs_s.at[level, p, s], rs_r.at[level, p, s], peer(p, level, s),
        )

    def ag(level, p, s, arriving):
        ks = [pos[a] for a in ORDERS[p][: level + 1]]
        if arriving:
            ks[level] = (ks[level] + 4 - s) % 4
        at = full.at[block_rows(ks), part_cols(p)]
        return remote(at, at, ag_s.at[level, p, s], ag_r.at[level, p, s], peer(p, level, s))

    def core_gather(p, s, c):
        k = along(p, 0, 4 - s)
        at = full.at[ds(c * HALF + k * 128, 128, 128), part_cols(p)]
        return remote(at, at, cg_s.at[p, s], cg_r.at[p, s], device(moved(c=1)))

    steps = OFFSETS + (0,)
    rescale = 1.0 / math.sqrt(TOTAL_MEM * TOTAL_CELLS)

    def run():
        begin()
        forward(0)
        forward(1)
        for o in range(1, 16):
            arrived(("area", o), area_arrival(o))
        receive_all("f", 0, FORECAST)
        pairwise(0)
        receive_all("f", 1, FORECAST)
        pairwise(1)
        receive_all("g", 0, BACK)
        backward(0)
        weight_gradients(0, 0)
        weight_gradients(0, 1)
        receive_all("g", 1, BACK)
        backward(1)
        weight_gradients(1, 1 - core)
        own_loss = jnp.sum(loss[...], keepdims=True)
        row = lax.broadcasted_iota(jnp.int32, (8, VP), 0)
        col = lax.broadcasted_iota(jnp.int32, (8, VP), 1)
        grad[0:8, H:WIDE] += jnp.where((row == 0) & (col == LOSS_COL), own_loss, 0.0)
        for s in steps:
            for p in range(3):
                start(("core", p, s), core_copy(s, p))
        weight_gradients(1, core)
        tiles = [(0, 0), (1, 0), (0, 1), (1, 1)]
        for n, s in enumerate(steps):
            for p in range(3):
                arrived(("core", p, s), core_copy(s, p))
                k = along(p, 0, s)
                rows, cols = block_rows([k]), part_cols(p)
                grad[rows, cols] += core_in[ds(k * 128, 128, 128), cols]
                if s:
                    start(("rs", 0, p, s), rs(0, p, s))
            embedding_derivative(*tiles[n])
        for p in range(3):
            for s in OFFSETS:
                arrived(("rs", 0, p, s), rs(0, p, s))
            rows = block_rows([along(p, 0, 0)])
            r1[p] = grad[rows, part_cols(p)] + s1[p, 0] + s1[p, 1] + s1[p, 2]
            for s in OFFSETS:
                start(("rs", 1, p, s), rs(1, p, s))
        for p in range(3):
            for s in OFFSETS:
                arrived(("rs", 1, p, s), rs(1, p, s))
            k = along(p, 1, 0)
            r2[p] = r1[p, ds(k * 32, 32, 32)] + s2[p, 0] + s2[p, 1] + s2[p, 2]
            for s in OFFSETS:
                start(("rs", 2, p, s), rs(2, p, s))
        for p in range(3):
            for s in OFFSETS:
                arrived(("rs", 2, p, s), rs(2, p, s))
            ks = [pos[a] for a in ORDERS[p]]
            total = r2[p, ds(ks[2] * 8, 8, 8)] + s3[p, 0] + s3[p, 1] + s3[p, 2]
            full[block_rows(ks), part_cols(p)] = total * rescale
            for s in OFFSETS:
                start(("ag", 2, p, s), ag(2, p, s, False))
        for level in (2, 1):
            for p in range(3):
                for s in OFFSETS:
                    arrived(("ag", level, p, s), ag(level, p, s, True))
                for s in OFFSETS:
                    start(("ag", level - 1, p, s), ag(level - 1, p, s, False))
                if level == 1:
                    start(("cg", p, 0), core_gather(p, 0, core))
        for s in (1, 3, 2):
            for p in range(3):
                arrived(("ag", 0, p, s), ag(0, p, s, True))
                start(("cg", p, s), core_gather(p, s, core))
        for s in (0, 1, 3, 2):
            for p in range(3):
                arrived(("cg", p, s), core_gather(p, s, 1 - core))

    run()
    for copy in sent.values():
        copy.wait_send()


def finish(ed, full, ed_out, grad_out, grad_t_out, penalty, sem):
    ed_copy = pltpu.make_async_copy(ed, ed_out, sem.at[0])
    ed_copy.start()
    grad_copy = pltpu.make_async_copy(full.at[:, 0:H], grad_out, sem.at[1])
    grad_copy.start()
    t = full[:, H:WIDE].T
    grad_t_out[0:VH] = t[0:VH]
    grad_t_out[VH:V] = t[64 : 64 + VH]
    rescale = 1.0 / math.sqrt(TOTAL_MEM * TOTAL_CELLS)
    at = full[0:1, H + LOSS_COL : H + LOSS_COL + 1]
    penalty[...] = at * (1.0 / (rescale * TOTAL_CELLS * V))
    ed_copy.wait()
    grad_copy.wait()


def per_device(
    embedding_tensor,
    first_projection_matrix,
    variable_projection_matrix,
    target,
    var_weight,
    area_weight,
):
    vmem = pl.BlockSpec(memory_space=pltpu.VMEM)
    hbm = pl.BlockSpec(memory_space=pl.ANY)
    dma = pltpu.SemaphoreType.DMA
    big = (MEM, H, CELLS)
    swap = (NQ, 8, MEM, VH, 128)
    in_vmem = (pltpu.VMEM(big, BF16), pltpu.VMEM((H, WIDE), F32))
    ed, full = pl.pallas_call(
        kernel,
        name="decoder_crps",
        out_shape=in_vmem,
        in_specs=[hbm, hbm, vmem, vmem, vmem, vmem],
        out_specs=(vmem, vmem),
        scratch_shapes=[
            pltpu.VMEM(big, BF16),
            pltpu.VMEM((H, H), BF16),
            pltpu.VMEM((H, H), BF16),
            pltpu.VMEM((H, VP), BF16),
            pltpu.VMEM((VP, H), BF16),
            pltpu.VMEM(big, BF16),
            pltpu.VMEM(big, F32),
            pltpu.VMEM((MEM, VP, CELLS), BF16),
            pltpu.VMEM(big, BF16),
            pltpu.VMEM((2, VH, CELLS), F32),
            pltpu.VMEM((2, VH, 128), F32),
            pltpu.VMEM((16, 8, 128), F32),
            pltpu.VMEM(swap, F32),
            pltpu.VMEM(swap, F32),
            pltpu.VMEM(swap, F32),
            pltpu.VMEM(swap, F32),
            pltpu.VMEM((H, WIDE), F32),
            pltpu.VMEM((HALF, WIDE), F32),
            pltpu.VMEM((3, 3, 128, PW), F32),
            pltpu.VMEM((3, 128, PW), F32),
            pltpu.VMEM((3, 3, 32, PW), F32),
            pltpu.VMEM((3, 32, PW), F32),
            pltpu.VMEM((3, 3, 8, PW), F32),
            pltpu.VMEM((8, 128), F32),
            dma((5,)),
            dma((16,)), dma((16,)),
            dma((NQ, 8)), dma((NQ, 8)),
            dma((NQ, 8)), dma((NQ, 8)),
            dma((4, 3)), dma((4, 3)),
            dma((3, 3, 4)), dma((3, 3, 4)),
            dma((3, 3, 4)), dma((3, 3, 4)),
            dma((3, 4)), dma((3, 4)),
        ],
        compiler_params=pltpu.CompilerParams(
            collective_id=0, has_side_effects=True, vmem_limit_bytes=50 * 2**20
        ),
        cost_estimate=pl.CostEstimate(
            flops=15_000_000_000, bytes_accessed=20_000_000, transcendentals=4_000_000
        ),
    )(
        embedding_tensor,
        first_projection_matrix,
        variable_projection_matrix.T,
        target,
        var_weight.reshape(1, V),
        area_weight.reshape(8, 128),
    )
    ed, grad_in, grad_out_t, penalty = pl.pallas_call(
        finish,
        name="write_out",
        out_shape=(
            jax.ShapeDtypeStruct(big, BF16),
            jax.ShapeDtypeStruct((H, H), F32),
            jax.ShapeDtypeStruct((V, H), F32),
            jax.ShapeDtypeStruct((1, 1), F32),
        ),
        in_specs=[vmem, vmem],
        out_specs=(hbm, hbm, vmem, vmem),
        scratch_shapes=[dma((2,))],
        compiler_params=pltpu.CompilerParams(vmem_limit_bytes=8 * 2**20),
    )(ed, full)
    return ed, grad_in, grad_out_t.T, penalty[0, 0]


def solution(mesh):
    in_specs = (P("member", None, "grid"), P(), P(), P(None, "grid"), P(), P("grid"))
    out_specs = (P("member", None, "grid"), P(), P(), P())
    return jax.shard_map(
        per_device, mesh=mesh, in_specs=in_specs, out_specs=out_specs, check_vma=False
    )
```

time: 101 us -> 89.3 us (0.88)
  local copies, waits for them, and re-layouts: 13.7 us -> 0 us
  Pallas kernels: 84.2 us -> 88.4 us
  between operations: 2.44 us -> 0.8 us
    slice x3 -> x0, local copies, waits for them, and re-layouts: 7.71 us -> none  [the longest x1 4.94 us: per_device(): return (ed, wide[:, :H], grad_out, crps)]
    unnamed x5 -> x0, local copies, waits for them, and re-layouts: 4.78 us -> none
    pallas_call x1 -> x2, Pallas kernels: 84.2 us -> 88.4 us  [the longest x1 84.2 us: per_device(): pl.pallas_call(kernel, name='decoder_crps', out_shape=in_vmem, in_specs=[...]
    reshape x1 -> x0, local copies, waits for them, and re-layouts: 1.17 us -> none  [per_device(): jnp.pad(var_weight, (0, VP - V)).reshape(1, VP)]
where the time goes in v2:
time: 89.3 us; the launch traced here: 89.2 us
  Pallas kernels  88.4 us (99%)
    pallas_call x1, Pallas kernels, per_device(): pl.pallas_call(kernel, name='decoder_crps', out_shape=in_vmem, in_specs=[...  84.2 us
    pallas_call x1, Pallas kernels, per_device(): pl.pallas_call(finish, name='write_out', out_shape=(jax.ShapeDtypeStruct(...  4.18 us

profile of v2, /device:TPU:1, one launch (start us, length us, event | category | flops | bytes accessed | tf_op | source)
XLA Modules:
  0.0 89.2 jit_solution(7037940901107417675)
XLA Ops:
  0.6 84.2 %decoder_crps.1 = (bf16[2,1024,1024]{2,1,0:T(8,128)(2,1)S(1)}, f32[1024,1152]{1,0:T(8,128)S(1)}) custom-call(bf16[2,1024,1024]{2,1,0:T(8,128)(2,1)} %emb.1, bf16[1024,1024]{1,0:T(8,128)(2,1)} %w1_hbm.1, bf16[100,1024]{1,0:T(8,128)(2,1)} %bitcast.6, bf16[100,1024]{1,0:T(8,128)(2,1)} %target.1, f32[1,100]{1,0:T(1,128)} %bitcast.8, f32[8,128]{1,0:T(8,128)} %bitcast.7), custom_call_target="tpu_custom_call" | custom-call | flops 15000000512 | bytes 20000000 | tf_op jit(solution)/shard_map/decoder_crps/pallas_call | solution.py:416
  84.9 4.2 %write_out.1 = (bf16[2,1024,1024]{2,1,0:T(8,128)(2,1)}, f32[1024,1024]{1,0:T(8,128)}, f32[100,1024]{1,0:T(8,128)}, f32[1,1]{1,0:T(1,128)}) custom-call(bf16[2,1024,1024]{2,1,0:T(8,128)(2,1)S(1)} %get-tuple-element.10.ed, f32[1024,1152]{1,0:T(8,128)S(1)} %get-tuple-element.11.full), custom_call_target="tpu_custom_call" | custom-call | tf_op jit(solution)/shard_map/write_out/pallas_call | solution.py:470

commit v3 on v2

v3 whole, which is shorter than its diff:
```python
import functools
import math

import jax
import jax.numpy as jnp
from jax import lax
from jax.experimental import pallas as pl
from jax.experimental.pallas import tpu as pltpu
from jax.sharding import PartitionSpec as P

SMOOTH_WIDTH = 0.1
ALPHA_FAIR = 0.95
MESH = pl.DeviceIdType.MESH
F32 = jnp.float32
BF16 = jnp.bfloat16
GELU_A = math.sqrt(2.0 / math.pi)
GELU_B = 0.044715

H = 1024
V = 100
CELLS = 1024
MEM = 2
TOTAL_MEM = 16
TOTAL_CELLS = 16384
NQ = 4
CQ = CELLS // NQ
NL = CQ // 128
NR = 8 // NL
VH = V // NR
VG = 128 // NR
VP = NR * VG
HALF = H // 2
WIDE = H + VP
NU = WIDE // 128
LOSS_COL = VH
ORDERS = (("x", "y", "z"), ("y", "z", "x"), ("z", "x", "y"))
OFFSETS = (2, 1, 3)


def dot(a, b):
    return lax.dot_general(a, b, (((1,), (0,)), ((), ())), preferred_element_type=F32)


def dot_t(a, b):
    return lax.dot_general(a, b, (((1,), (1,)), ((), ())), preferred_element_type=F32)


def gelu_and_derivative(x):
    x2 = x * x
    t = jnp.tanh(x * (GELU_A + (GELU_A * GELU_B) * x2))
    h = 0.5 + 0.5 * t
    y = x * h
    return y, h + (y * (1.0 - t)) * (GELU_A + (3.0 * GELU_A * GELU_B) * x2)


def ds(start, size, multiple):
    return pl.ds(pl.multiple_of(start, multiple), size)


def kernel(
    emb, w1_hbm, w2_hbm, target_hbm, vw_hbm, aw_hbm,
    ed, full,
    e, w1, w1t, w2_in, target, vw, aw, w2p, w2t, act, dg, gv, gp, tgt, vcol, av,
    fs, fr, gs, gr, grad, core_in, s1, r1, s2, s3, loss,
    in_sem, area_sem, f_sem, g_sem, core_sem, rs0_sem, rs1_sem, x_sem, ag1_sem, ag0_sem, cg_sem,
):
    me = lax.axis_index("member")
    g = lax.axis_index("grid")
    pos = {"x": me % 4, "y": (g // 8) * 2 + me // 4, "z": (g // 2) % 4, "c": g % 2}
    core = pos["c"]

    def device(p):
        return ((p["y"] % 2) * 4 + p["x"], ((p["y"] // 2) * 4 + p["z"]) * 2 + p["c"])

    def moved(**by):
        return {k: (v + by[k]) % (2 if k == "c" else 4) if k in by else v for k, v in pos.items()}

    def remote(src, dst, send_sem, recv_sem, to):
        return pltpu.make_async_remote_copy(
            src_ref=src, dst_ref=dst, send_sem=send_sem, recv_sem=recv_sem,
            device_id=to, device_id_type=MESH,
        )

    other_core = device(moved(c=1))

    def arrived(ref, sem):
        remote(ref, ref, sem, sem, other_core).wait_recv()

    def left(ref, sem):
        remote(ref, ref, sem, sem, other_core).wait_send()

    def member_peer(o):
        return (me // 4 + o // 4) % 2 * 4 + (me % 4 + o % 4) % 4

    def emb_copy(q):
        sl = pl.ds(q * CQ, CQ)
        return pltpu.make_async_copy(emb.at[:, :, sl], e.at[:, :, sl], in_sem.at[q])

    w1_copy = pltpu.make_async_copy(w1_hbm, w1, in_sem.at[NQ])
    small_copies = [
        pltpu.make_async_copy(src, dst, in_sem.at[NQ + 1 + i])
        for i, (src, dst) in enumerate(
            ((w2_hbm, w2_in), (target_hbm, target), (vw_hbm, vw), (aw_hbm, aw))
        )
    ]
    barrier = pltpu.get_barrier_semaphore()

    def load():
        w1_copy.start()
        for copy in small_copies:
            copy.start()
        for q in range(NQ):
            emb_copy(q).start()

    def greet():
        peers = [(member_peer(o), g) for o in range(1, 8)]
        peers += [(me, (g + o) % 16) for o in range(1, 16)]
        peers += [((me + 4) % 8, (g + 8) % 16)]
        for peer in peers:
            pl.semaphore_signal(barrier, inc=1, device_id=peer, device_id_type=MESH)

    def small_operands():
        for copy in small_copies:
            copy.wait()
        wide = w2_in[...].astype(F32)
        gap = jnp.zeros((VG - VH, H), F32)
        groups = []
        for r in range(NR):
            groups += [wide[r * VH : r * VH + VH], gap]
        w2t[...] = jnp.concatenate(groups, axis=0).astype(BF16)
        w2p[...] = w2t[...].T
        t32 = target[...].astype(F32)
        columns = jnp.broadcast_to(vw[...], (128, V)).T
        for r in range(NR):
            tgt[r] = t32[r * VH : r * VH + VH]
            vcol[r] = columns[r * VH : r * VH + VH]
        av[g] = aw[...]
        loss[...] = jnp.zeros_like(loss)

    def send_area():
        for o in range(1, 16):
            remote(
                av.at[g], av.at[g], area_sem.at[0], area_sem.at[1], (me, (g + o) % 16)
            ).start()

    PEERS = (6, 2, 5, 7, 4, 1, 3)

    def send_all(q, src, dst, sem):
        for o in PEERS:
            peer = member_peer(o)
            remote(src.at[q, peer], dst.at[q, me], sem.at[NQ], sem.at[q], (peer, g)).start()
        dst[q, me] = src[q, me]

    def receive_all(q, dst, sem):
        arrived(dst.at[q, pl.ds(0, 7)], sem.at[q])

    def forward(q):
        sl = pl.ds(q * CQ, CQ)
        emb_copy(q).wait()

        @pl.loop(0, MEM)
        def _(m):
            y, d = gelu_and_derivative(dot(w1t[...], e[m, :, sl]))
            act[m, :, sl] = y.astype(BF16)
            dg[m, :, sl] = d
            fc = dot(w2t[...], act[m, :, sl])
            for r in range(NR):
                for l in range(NL):
                    fs[q, r * NL + l, m] = fc[VG * r : VG * r + VH, 128 * l : 128 * l + 128]

    coef = (1.0 - (1.0 - ALPHA_FAIR) / TOTAL_MEM) / (TOTAL_MEM - 1)
    d2 = SMOOTH_WIDTH * SMOOTH_WIDTH

    def pairwise(q):
        mine_r, mine_l = me // NL, me % NL
        lanes = ds(q * CQ + mine_l * 128, 128, 128)
        mean = jnp.sum(jnp.sum(av[...], axis=0), keepdims=True) / TOTAL_CELLS
        area = aw[pl.ds(q * NL + mine_l, 1), :] / mean

        def tile(rows, n):
            scale = area * vcol[mine_r, rows, :]
            t = tgt[mine_r, rows, lanes]
            f = [fr[q, k // 2, k % 2, rows, :] for k in range(TOTAL_MEM)]
            s = [None] * TOTAL_MEM
            spread = None
            for i in range(TOTAL_MEM):
                for k in range(i + 1, TOTAL_MEM):
                    d = f[i] - f[k]
                    w = d * d + d2
                    inv = lax.rsqrt(w)
                    slope = d * inv
                    s[i] = slope if s[i] is None else s[i] + slope
                    s[k] = -slope if s[k] is None else s[k] - slope
                    smooth = w * inv - SMOOTH_WIDTH
                    spread = smooth if spread is None else spread + smooth
            truth = None
            for i in range(TOTAL_MEM):
                d = f[i] - t
                w = d * d + d2
                inv = lax.rsqrt(w)
                gs[q, i // 2, i % 2, rows, :] = scale * (d * inv - coef * s[i])
                smooth = w * inv - SMOOTH_WIDTH
                truth = smooth if truth is None else truth + smooth
            loss[0:n, :] += scale * (truth / TOTAL_MEM - (coef / TOTAL_MEM) * spread)

        @pl.loop(0, VH // 8)
        def _(i):
            tile(ds(i * 8, 8, 8), 8)

        tile(pl.ds(VH // 8 * 8, VH % 8), VH % 8)

    def backward(q):
        sl = pl.ds(q * CQ, CQ)
        gap = jnp.zeros((VG - VH, 128), F32)

        @pl.loop(0, MEM)
        def _(m):
            for l in range(NL):
                groups = []
                for r in range(NR):
                    groups += [gr[q, r * NL + l, m], gap]
                at = q * CQ + 128 * l
                gv[m, :, at : at + 128] = jnp.concatenate(groups, axis=0).astype(BF16)
            gp[m, :, sl] = (dot(w2p[...], gv[m, :, sl]) * dg[m, :, sl]).astype(BF16)

    def add_to_grad(rows, cols, new, first):
        if first:
            grad[rows, cols] = new
        else:
            grad[rows, cols] += new

    def grad_in_tile(sl, half, j, first):
        rows, cols = ds(half * HALF, HALF, HALF), ds(j * 256, 256, 256)
        new = dot_t(e[0, rows, sl], gp[0, cols, sl]) + dot_t(e[1, rows, sl], gp[1, cols, sl])
        add_to_grad(rows, cols, new, first)

    def grad_out_tile(sl, half, first):
        rows = ds(half * HALF, HALF, HALF)
        new = dot_t(act[0, rows, sl], gv[0, :, sl]) + dot_t(act[1, rows, sl], gv[1, :, sl])
        add_to_grad(rows, pl.ds(H, VP), new, first)

    def weight_gradients(q, n, half):
        sl = pl.ds(q * CQ, n * CQ)

        @pl.loop(0, 4)
        def _(j):
            grad_in_tile(sl, half, j, q == 0)

        grad_out_tile(sl, half, q == 0)

    def embedding_derivative(m, q):
        sl = pl.ds(q * 512, 512)
        ed[m, :, sl] = dot(w1[...], gp[m, :, sl]).astype(BF16)

    def cols_of(u):
        return pl.ds(u * 128, 128)

    def along(u, level, s):
        return (pos[ORDERS[u % 3][level]] + s) % 4

    def peer_of(u, level, s):
        return device(moved(**{ORDERS[u % 3][level]: s}))

    def block_rows(ks):
        begin = core * HALF
        for k, size in zip(ks, (128, 32)):
            begin = begin + k * size
        size = (128, 32)[len(ks) - 1]
        return ds(begin, size, size)

    def core_send(u):
        remote(
            grad.at[ds((1 - core) * HALF, HALF, HALF), cols_of(u)], core_in.at[:, cols_of(u)],
            core_sem.at[NU], core_sem.at[u], other_core,
        ).start()

    def core_receive(u):
        cols = cols_of(u)
        arrived(core_in.at[:, cols], core_sem.at[u])
        grad[ds(core * HALF, HALF, HALF), cols] += core_in[:, cols]
        for s in OFFSETS:
            k = along(u, 0, s)
            remote(
                grad.at[block_rows([k]), cols], s1.at[u, s - 1],
                rs0_sem.at[NU], rs0_sem.at[u], peer_of(u, 0, s),
            ).start()

    def rs0_receive(u):
        arrived(s1.at[u], rs0_sem.at[u])
        own = grad[block_rows([along(u, 0, 0)]), cols_of(u)]
        r1[u] = own + s1[u, 0] + s1[u, 1] + s1[u, 2]
        for s in OFFSETS:
            k = along(u, 1, s)
            remote(
                r1.at[u, ds(k * 32, 32, 32)], s2.at[u, s - 1],
                rs1_sem.at[NU], rs1_sem.at[u], peer_of(u, 1, s),
            ).start()

    def rs1_receive(u):
        arrived(s2.at[u], rs1_sem.at[u])
        own = r1[u, ds(along(u, 1, 0) * 32, 32, 32)]
        k = along(u, 2, 0)
        s3[u, k] = own + s2[u, 0] + s2[u, 1] + s2[u, 2]
        for s in OFFSETS:
            remote(
                s3.at[u, k], s3.at[u, k], x_sem.at[NU], x_sem.at[u], peer_of(u, 2, s)
            ).start()

    rescale = 1.0 / math.sqrt(TOTAL_MEM * TOTAL_CELLS)

    def x_receive(u):
        arrived(s3.at[u, pl.ds(0, 3)], x_sem.at[u])
        at = (block_rows([along(u, 0, 0), along(u, 1, 0)]), cols_of(u))
        full[at] = (s3[u, 0] + s3[u, 1] + s3[u, 2] + s3[u, 3]) * rescale
        for s in OFFSETS:
            remote(
                full.at[at], full.at[at], ag1_sem.at[NU], ag1_sem.at[u], peer_of(u, 1, s)
            ).start()

    def to_core(u, s):
        at = (block_rows([along(u, 0, s)]), cols_of(u))
        remote(full.at[at], full.at[at], cg_sem.at[NU], cg_sem.at[u], other_core).start()

    def ag1_receive(u):
        arrived(full.at[pl.ds(0, 96), cols_of(u)], ag1_sem.at[u])
        at = (block_rows([along(u, 0, 0)]), cols_of(u))
        for s in OFFSETS:
            remote(
                full.at[at], full.at[at], ag0_sem.at[NU], ag0_sem.at[u], peer_of(u, 0, s)
            ).start()
        to_core(u, 0)

    def ag0_receive(u):
        arrived(full.at[pl.ds(0, 384), cols_of(u)], ag0_sem.at[u])
        for s in OFFSETS:
            to_core(u, s)

    def cg_receive(u):
        arrived(full.at[pl.ds(0, HALF), cols_of(u)], cg_sem.at[u])

    def run():
        load()
        greet()
        small_operands()
        w1_copy.wait()
        w1t[...] = w1[...].T
        forward(0)
        pl.semaphore_wait(barrier, 23)
        send_area()
        send_all(0, fs, fr, f_sem)
        forward(1)
        send_all(1, fs, fr, f_sem)
        forward(2)
        send_all(2, fs, fr, f_sem)
        arrived(av.at[pl.ds(0, 15)], area_sem.at[1])
        receive_all(0, fr, f_sem)
        pairwise(0)
        send_all(0, gs, gr, g_sem)
        forward(3)
        send_all(3, fs, fr, f_sem)
        receive_all(1, fr, f_sem)
        pairwise(1)
        send_all(1, gs, gr, g_sem)
        receive_all(2, fr, f_sem)
        pairwise(2)
        send_all(2, gs, gr, g_sem)
        receive_all(0, gr, g_sem)
        backward(0)
        receive_all(3, fr, f_sem)
        pairwise(3)
        send_all(3, gs, gr, g_sem)
        receive_all(1, gr, g_sem)
        backward(1)
        weight_gradients(0, 2, 0)
        weight_gradients(0, 2, 1)
        receive_all(2, gr, g_sem)
        backward(2)
        weight_gradients(2, 1, 0)
        weight_gradients(2, 1, 1)
        receive_all(3, gr, g_sem)
        backward(3)
        own_loss = jnp.sum(loss[...], keepdims=True)
        row = lax.broadcasted_iota(jnp.int32, (8, VP), 0)
        col = lax.broadcasted_iota(jnp.int32, (8, VP), 1)
        grad[0:8, H:WIDE] += jnp.where((row == 0) & (col == LOSS_COL), own_loss, 0.0)
        last = pl.ds(3 * CQ, CQ)
        for j in range(4):
            grad_in_tile(last, 1 - core, j, False)
            core_send(2 * j)
            core_send(2 * j + 1)
        grad_out_tile(last, 1 - core, False)
        core_send(NU - 1)
        weight_gradients(3, 1, core)
        waves = ((0, 1, 2), (3, 4, 5), (6, 7, 8))

        def each(step, wave):
            for u in waves[wave]:
                step(u)

        each(core_receive, 0)
        embedding_derivative(0, 0)
        each(core_receive, 1)
        embedding_derivative(1, 0)
        each(core_receive, 2)
        each(rs0_receive, 0)
        embedding_derivative(0, 1)
        each(rs0_receive, 1)
        each(rs1_receive, 0)
        embedding_derivative(1, 1)
        each(rs0_receive, 2)
        each(rs1_receive, 1)
        each(x_receive, 0)
        each(rs1_receive, 2)
        each(x_receive, 1)
        each(ag1_receive, 0)
        each(x_receive, 2)
        each(ag1_receive, 1)
        each(ag1_receive, 2)
        each(ag0_receive, 0)
        each(ag0_receive, 1)
        each(ag0_receive, 2)
        for wave in range(3):
            each(cg_receive, wave)

    run()
    left(av.at[pl.ds(0, 15)], area_sem.at[0])
    left(fs.at[:, pl.ds(0, 7)], f_sem.at[NQ])
    left(gs.at[:, pl.ds(0, 7)], g_sem.at[NQ])
    left(core_in, core_sem.at[NU])
    left(s1, rs0_sem.at[NU])
    left(s2, rs1_sem.at[NU])
    left(s3.at[:, pl.ds(0, 3)], x_sem.at[NU])
    left(s2, ag1_sem.at[NU])
    left(s1, ag0_sem.at[NU])
    left(core_in, cg_sem.at[NU])


def finish(ed, full, ed_out, grad_out, grad_t_out, penalty, sem):
    ed_copy = pltpu.make_async_copy(ed, ed_out, sem.at[0])
    ed_copy.start()
    grad_copy = pltpu.make_async_copy(full.at[:, 0:H], grad_out, sem.at[1])
    grad_copy.start()
    t = full[:, H:WIDE].T
    grad_t_out[...] = jnp.concatenate([t[VG * r : VG * r + VH] for r in range(NR)], axis=0)
    rescale = 1.0 / math.sqrt(TOTAL_MEM * TOTAL_CELLS)
    at = full[0:1, H + LOSS_COL : H + LOSS_COL + 1]
    penalty[...] = at * (1.0 / (rescale * TOTAL_CELLS * V))
    ed_copy.wait()
    grad_copy.wait()


def per_device(
    embedding_tensor,
    first_projection_matrix,
    variable_projection_matrix,
    target,
    var_weight,
    area_weight,
):
    vmem = pl.BlockSpec(memory_space=pltpu.VMEM)
    hbm = pl.BlockSpec(memory_space=pl.ANY)
    dma = pltpu.SemaphoreType.DMA
    big = (MEM, H, CELLS)
    swap = (NQ, 8, MEM, VH, 128)
    in_vmem = (pltpu.VMEM(big, BF16), pltpu.VMEM((H, WIDE), F32))
    ed, full = pl.pallas_call(
        kernel,
        name="decoder_crps",
        out_shape=in_vmem,
        in_specs=[hbm] * 6,
        out_specs=(vmem, vmem),
        scratch_shapes=[
            pltpu.VMEM(big, BF16),
            pltpu.VMEM((H, H), BF16),
            pltpu.VMEM((H, H), BF16),
            pltpu.VMEM((V, H), BF16),
            pltpu.VMEM((V, CELLS), BF16),
            pltpu.VMEM((1, V), F32),
            pltpu.VMEM((8, 128), F32),
            pltpu.VMEM((H, VP), BF16),
            pltpu.VMEM((VP, H), BF16),
            pltpu.VMEM(big, BF16),
            pltpu.VMEM(big, F32),
            pltpu.VMEM((MEM, VP, CELLS), BF16),
            pltpu.VMEM(big, BF16),
            pltpu.VMEM((NR, VH, CELLS), F32),
            pltpu.VMEM((NR, VH, 128), F32),
            pltpu.VMEM((16, 8, 128), F32),
            pltpu.VMEM(swap, F32),
            pltpu.VMEM(swap, F32),
            pltpu.VMEM(swap, F32),
            pltpu.VMEM(swap, F32),
            pltpu.VMEM((H, WIDE), F32),
            pltpu.VMEM((HALF, WIDE), F32),
            pltpu.VMEM((NU, 3, 128, 128), F32),
            pltpu.VMEM((NU, 128, 128), F32),
            pltpu.VMEM((NU, 3, 32, 128), F32),
            pltpu.VMEM((NU, 4, 32, 128), F32),
            pltpu.VMEM((8, 128), F32),
            dma((NQ + 5,)),
            dma((2,)),
            dma((NQ + 1,)), dma((NQ + 1,)),
            dma((NU + 1,)), dma((NU + 1,)), dma((NU + 1,)), dma((NU + 1,)),
            dma((NU + 1,)), dma((NU + 1,)), dma((NU + 1,)),
        ],
        compiler_params=pltpu.CompilerParams(
            collective_id=0, has_side_effects=True, vmem_limit_bytes=50 * 2**20
        ),
        cost_estimate=pl.CostEstimate(
            flops=15_000_000_000, bytes_accessed=20_000_000, transcendentals=4_000_000
        ),
    )(
        embedding_tensor,
        first_projection_matrix,
        variable_projection_matrix.T,
        target,
        var_weight.reshape(1, V),
        area_weight.reshape(8, 128),
    )
    ed, grad_in, grad_out_t, penalty = pl.pallas_call(
        finish,
        name="write_out",
        out_shape=(
            jax.ShapeDtypeStruct(big, BF16),
            jax.ShapeDtypeStruct((H, H), F32),
            jax.ShapeDtypeStruct((V, H), F32),
            jax.ShapeDtypeStruct((1, 1), F32),
        ),
        in_specs=[vmem, vmem],
        out_specs=(hbm, hbm, vmem, vmem),
        scratch_shapes=[dma((2,))],
        compiler_params=pltpu.CompilerParams(vmem_limit_bytes=8 * 2**20),
    )(ed, full)
    return ed, grad_in, grad_out_t.T, penalty[0, 0]


def solution(mesh):
    in_specs = (P("member", None, "grid"), P(), P(), P(None, "grid"), P(), P("grid"))
    out_specs = (P("member", None, "grid"), P(), P(), P())
    return jax.shard_map(
        per_device, mesh=mesh, in_specs=in_specs, out_specs=out_specs, check_vma=False
    )
```

time: 89.3 us -> 79.8 us (0.89)
  Pallas kernels: 88.4 us -> 78.9 us
    pallas_call x1, Pallas kernels: 84.2 us -> 74.7 us  [per_device(): pl.pallas_call(kernel, name='decoder_crps', out_shape=in_vmem, in_specs=[...]
where the time goes in v3:
time: 79.8 us; the launch traced here: 79.7 us
  Pallas kernels  78.9 us (99%)
  between operations  0.8 us (1%)
    pallas_call x1, Pallas kernels, per_device(): pl.pallas_call(kernel, name='decoder_crps', out_shape=in_vmem, in_specs=[...  74.7 us
    pallas_call x1, Pallas kernels, per_device(): pl.pallas_call(finish, name='write_out', out_shape=(jax.ShapeDtypeStruct(...  4.18 us

profile of v3, /device:TPU:1, one launch (start us, length us, event | category | flops | bytes accessed | tf_op | source)
XLA Modules:
  0.0 79.7 jit_solution(16359199407685268557)
XLA Ops:
  0.6 74.7 %decoder_crps.1 = (bf16[2,1024,1024]{2,1,0:T(8,128)(2,1)S(1)}, f32[1024,1152]{1,0:T(8,128)S(1)}) custom-call(bf16[2,1024,1024]{2,1,0:T(8,128)(2,1)} %emb.1, bf16[1024,1024]{1,0:T(8,128)(2,1)} %w1_hbm.1, bf16[100,1024]{1,0:T(8,128)(2,1)} %bitcast.6, bf16[100,1024]{1,0:T(8,128)(2,1)} %target_hbm.1, f32[1,100]{1,0:T(1,128)} %bitcast.8, f32[8,128]{1,0:T(8,128)} %bitcast.7), custom_call_target="tpu_custom_call" | custom-call | flops 15000000512 | bytes 20000000 | tf_op jit(solution)/shard_map/decoder_crps/pallas_call | solution.py:466
  75.3 4.2 %write_out.1 = (bf16[2,1024,1024]{2,1,0:T(8,128)(2,1)}, f32[1024,1024]{1,0:T(8,128)}, f32[100,1024]{1,0:T(8,128)}, f32[1,1]{1,0:T(1,128)}) custom-call(bf16[2,1024,1024]{2,1,0:T(8,128)(2,1)S(1)} %get-tuple-element.10.ed, f32[1024,1152]{1,0:T(8,128)S(1)} %get-tuple-element.11.full), custom_call_target="tpu_custom_call" | custom-call | tf_op jit(solution)/shard_map/write_out/pallas_call | solution.py:520

commit v4 on v3

--- a/solution.py
+++ b/solution.py
@@ -346,8 +346,8 @@
         w1t[...] = w1[...].T
         forward(0)
         pl.semaphore_wait(barrier, 23)
+        send_all(0, fs, fr, f_sem)
         send_area()
-        send_all(0, fs, fr, f_sem)
         forward(1)
         send_all(1, fs, fr, f_sem)
         forward(2)
@@ -375,33 +375,41 @@
         weight_gradients(0, 2, 1)
         receive_all(2, gr, g_sem)
         backward(2)
-        weight_gradients(2, 1, 0)
-        weight_gradients(2, 1, 1)
         receive_all(3, gr, g_sem)
         backward(3)
         own_loss = jnp.sum(loss[...], keepdims=True)
         row = lax.broadcasted_iota(jnp.int32, (8, VP), 0)
         col = lax.broadcasted_iota(jnp.int32, (8, VP), 1)
         grad[0:8, H:WIDE] += jnp.where((row == 0) & (col == LOSS_COL), own_loss, 0.0)
-        last = pl.ds(3 * CQ, CQ)
+        last = pl.ds(2 * CQ, 2 * CQ)
         for j in range(4):
             grad_in_tile(last, 1 - core, j, False)
             core_send(2 * j)
             core_send(2 * j + 1)
         grad_out_tile(last, 1 - core, False)
         core_send(NU - 1)
-        weight_gradients(3, 1, core)
+        grad_in_tile(last, core, 0, False)
+        core_receive(0)
+        grad_in_tile(last, core, 1, False)
+        core_receive(1)
+        grad_in_tile(last, core, 2, False)
+        core_receive(2)
+        core_receive(3)
+        grad_in_tile(last, core, 3, False)
+        core_receive(4)
+        grad_out_tile(last, core, False)
+        core_receive(5)
+        embedding_derivative(0, 0)
+        core_receive(6)
+        core_receive(7)
+        core_receive(8)
         waves = ((0, 1, 2), (3, 4, 5), (6, 7, 8))
 
         def each(step, wave):
             for u in waves[wave]:
                 step(u)
 
-        each(core_receive, 0)
-        embedding_derivative(0, 0)
-        each(core_receive, 1)
         embedding_derivative(1, 0)
-        each(core_receive, 2)
         each(rs0_receive, 0)
         embedding_derivative(0, 1)
         each(rs0_receive, 1)

time: 79.8 us -> 78 us (0.977)
  Pallas kernels: 78.9 us -> 77.1 us
    pallas_call x1, Pallas kernels: 74.7 us -> 72.9 us  [per_device(): pl.pallas_call(kernel, name='decoder_crps', out_shape=in_vmem, in_specs=[...]
where the time goes in v4:
time: 78 us; the launch traced here: 77.9 us
  Pallas kernels  77.1 us (99%)
  between operations  0.8 us (1%)
    pallas_call x1, Pallas kernels, per_device(): pl.pallas_call(kernel, name='decoder_crps', out_shape=in_vmem, in_specs=[...  72.9 us
    pallas_call x1, Pallas kernels, per_device(): pl.pallas_call(finish, name='write_out', out_shape=(jax.ShapeDtypeStruct(...  4.18 us

profile of v4, /device:TPU:1, one launch (start us, length us, event | category | flops | bytes accessed | tf_op | source)
XLA Modules:
  0.0 77.9 jit_solution(10115586761183647001)
XLA Ops:
  0.6 72.9 %decoder_crps.1 = (bf16[2,1024,1024]{2,1,0:T(8,128)(2,1)S(1)}, f32[1024,1152]{1,0:T(8,128)S(1)}) custom-call(bf16[2,1024,1024]{2,1,0:T(8,128)(2,1)} %emb.1, bf16[1024,1024]{1,0:T(8,128)(2,1)} %w1_hbm.1, bf16[100,1024]{1,0:T(8,128)(2,1)} %bitcast.6, bf16[100,1024]{1,0:T(8,128)(2,1)} %target_hbm.1, f32[1,100]{1,0:T(1,128)} %bitcast.8, f32[8,128]{1,0:T(8,128)} %bitcast.7), custom_call_target="tpu_custom_call" | custom-call | flops 15000000512 | bytes 20000000 | tf_op jit(solution)/shard_map/decoder_crps/pallas_call | solution.py:474
  73.5 4.2 %write_out.1 = (bf16[2,1024,1024]{2,1,0:T(8,128)(2,1)}, f32[1024,1024]{1,0:T(8,128)}, f32[100,1024]{1,0:T(8,128)}, f32[1,1]{1,0:T(1,128)}) custom-call(bf16[2,1024,1024]{2,1,0:T(8,128)(2,1)S(1)} %get-tuple-element.10.ed, f32[1024,1152]{1,0:T(8,128)S(1)} %get-tuple-element.11.full), custom_call_target="tpu_custom_call" | custom-call | tf_op jit(solution)/shard_map/write_out/pallas_call | solution.py:528

commit v5 on v4

--- a/solution.py
+++ b/solution.py
@@ -158,8 +158,7 @@
         sl = pl.ds(q * CQ, CQ)
         emb_copy(q).wait()
 
-        @pl.loop(0, MEM)
-        def _(m):
+        for m in range(MEM):
             y, d = gelu_and_derivative(dot(w1t[...], e[m, :, sl]))
             act[m, :, sl] = y.astype(BF16)
             dg[m, :, sl] = d
@@ -203,18 +202,14 @@
                 truth = smooth if truth is None else truth + smooth
             loss[0:n, :] += scale * (truth / TOTAL_MEM - (coef / TOTAL_MEM) * spread)
 
-        @pl.loop(0, VH // 8)
-        def _(i):
-            tile(ds(i * 8, 8, 8), 8)
-
-        tile(pl.ds(VH // 8 * 8, VH % 8), VH % 8)
+        for i in range(0, VH, 8):
+            tile(pl.ds(i, min(8, VH - i)), min(8, VH - i))
 
     def backward(q):
         sl = pl.ds(q * CQ, CQ)
         gap = jnp.zeros((VG - VH, 128), F32)
 
-        @pl.loop(0, MEM)
-        def _(m):
+        for m in range(MEM):
             for l in range(NL):
                 groups = []
                 for r in range(NR):
@@ -242,8 +237,7 @@
     def weight_gradients(q, n, half):
         sl = pl.ds(q * CQ, n * CQ)
 
-        @pl.loop(0, 4)
-        def _(j):
+        for j in range(4):
             grad_in_tile(sl, half, j, q == 0)
 
         grad_out_tile(sl, half, q == 0)
@@ -399,22 +393,19 @@
         core_receive(4)
         grad_out_tile(last, core, False)
         core_receive(5)
-        embedding_derivative(0, 0)
-        core_receive(6)
-        core_receive(7)
-        core_receive(8)
         waves = ((0, 1, 2), (3, 4, 5), (6, 7, 8))
 
         def each(step, wave):
             for u in waves[wave]:
                 step(u)
 
+        embedding_derivative(0, 0)
+        each(rs0_receive, 0)
+        each(core_receive, 2)
         embedding_derivative(1, 0)
-        each(rs0_receive, 0)
-        embedding_derivative(0, 1)
         each(rs0_receive, 1)
         each(rs1_receive, 0)
-        embedding_derivative(1, 1)
+        embedding_derivative(0, 1)
         each(rs0_receive, 2)
         each(rs1_receive, 1)
         each(x_receive, 0)
@@ -422,6 +413,7 @@
         each(x_receive, 1)
         each(ag1_receive, 0)
         each(x_receive, 2)
+        embedding_derivative(1, 1)
         each(ag1_receive, 1)
         each(ag1_receive, 2)
         each(ag0_receive, 0)

time: 78 us -> 74.9 us (0.960)
  Pallas kernels: 77.1 us -> 73.9 us
    pallas_call x1, Pallas kernels: 72.9 us -> 69.8 us  [per_device(): pl.pallas_call(kernel, name='decoder_crps', out_shape=in_vmem, in_specs=[...]
where the time goes in v5:
time: 74.9 us; the launch traced here: 74.8 us
  Pallas kernels  73.9 us (99%)
  between operations  0.8 us (1%)
    pallas_call x1, Pallas kernels, per_device(): pl.pallas_call(kernel, name='decoder_crps', out_shape=in_vmem, in_specs=[...  69.8 us
    pallas_call x1, Pallas kernels, per_device(): pl.pallas_call(finish, name='write_out', out_shape=(jax.ShapeDtypeStruct(...  4.18 us

profile of v5, /device:TPU:1, one launch (start us, length us, event | category | flops | bytes accessed | tf_op | source)
XLA Modules:
  0.0 74.8 jit_solution(2878025397140219356)
XLA Ops:
  0.6 69.8 %decoder_crps.1 = (bf16[2,1024,1024]{2,1,0:T(8,128)(2,1)S(1)}, f32[1024,1152]{1,0:T(8,128)S(1)}) custom-call(bf16[2,1024,1024]{2,1,0:T(8,128)(2,1)} %emb.1, bf16[1024,1024]{1,0:T(8,128)(2,1)} %w1_hbm.1, bf16[100,1024]{1,0:T(8,128)(2,1)} %bitcast.6, bf16[100,1024]{1,0:T(8,128)(2,1)} %target_hbm.1, f32[1,100]{1,0:T(1,128)} %bitcast.8, f32[8,128]{1,0:T(8,128)} %bitcast.7), custom_call_target="tpu_custom_call" | custom-call | flops 15000000512 | bytes 20000000 | tf_op jit(solution)/shard_map/decoder_crps/pallas_call | solution.py:466
  70.4 4.2 %write_out.1 = (bf16[2,1024,1024]{2,1,0:T(8,128)(2,1)}, f32[1024,1024]{1,0:T(8,128)}, f32[100,1024]{1,0:T(8,128)}, f32[1,1]{1,0:T(1,128)}) custom-call(bf16[2,1024,1024]{2,1,0:T(8,128)(2,1)S(1)} %get-tuple-element.10.ed, f32[1024,1152]{1,0:T(8,128)S(1)} %get-tuple-element.11.full), custom_call_target="tpu_custom_call" | custom-call | tf_op jit(solution)/shard_map/write_out/pallas_call | solution.py:520

commit v6 on v5

--- a/solution.py
+++ b/solution.py
@@ -106,9 +106,9 @@
     barrier = pltpu.get_barrier_semaphore()
 
     def load():
-        w1_copy.start()
         for copy in small_copies:
             copy.start()
+        w1_copy.start()
         for q in range(NQ):
             emb_copy(q).start()
 
@@ -154,11 +154,19 @@
     def receive_all(q, dst, sem):
         arrived(dst.at[q, pl.ds(0, 7)], sem.at[q])
 
-    def forward(q):
+    def send_member(q, m):
+        for o in PEERS:
+            peer = member_peer(o)
+            remote(
+                fs.at[q, peer, m], fr.at[q, me, m], f_sem.at[NQ], f_sem.at[q], (peer, g)
+            ).start()
+        fr[q, me, m] = fs[q, me, m]
+
+    def forward(q, members=range(MEM)):
         sl = pl.ds(q * CQ, CQ)
-        emb_copy(q).wait()
-
-        for m in range(MEM):
+        if 0 in members:
+            emb_copy(q).wait()
+        for m in members:
             y, d = gelu_and_derivative(dot(w1t[...], e[m, :, sl]))
             act[m, :, sl] = y.astype(BF16)
             dg[m, :, sl] = d
@@ -338,9 +346,11 @@
         small_operands()
         w1_copy.wait()
         w1t[...] = w1[...].T
-        forward(0)
+        forward(0, (0,))
         pl.semaphore_wait(barrier, 23)
-        send_all(0, fs, fr, f_sem)
+        send_member(0, 0)
+        forward(0, (1,))
+        send_member(0, 1)
         send_area()
         forward(1)
         send_all(1, fs, fr, f_sem)
@@ -405,7 +415,6 @@
         embedding_derivative(1, 0)
         each(rs0_receive, 1)
         each(rs1_receive, 0)
-        embedding_derivative(0, 1)
         each(rs0_receive, 2)
         each(rs1_receive, 1)
         each(x_receive, 0)
@@ -413,10 +422,11 @@
         each(x_receive, 1)
         each(ag1_receive, 0)
         each(x_receive, 2)
-        embedding_derivative(1, 1)
         each(ag1_receive, 1)
         each(ag1_receive, 2)
+        embedding_derivative(0, 1)
         each(ag0_receive, 0)
+        embedding_derivative(1, 1)
         each(ag0_receive, 1)
         each(ag0_receive, 2)
         for wave in range(3):

time: 74.9 us -> 75.2 us (level)
  no operation moved by 1% of the time
where the time goes in v6:
time: 75.2 us; the launch traced here: 75.1 us
  Pallas kernels  74.3 us (99%)
  between operations  0.8 us (1%)
    pallas_call x1, Pallas kernels, per_device(): pl.pallas_call(kernel, name='decoder_crps', out_shape=in_vmem, in_specs=[...  70.1 us
    pallas_call x1, Pallas kernels, per_device(): pl.pallas_call(finish, name='write_out', out_shape=(jax.ShapeDtypeStruct(...  4.18 us

profile of v6, /device:TPU:1, one launch (start us, length us, event | category | flops | bytes accessed | tf_op | source)
XLA Modules:
  0.0 75.1 jit_solution(1193481692474422746)
XLA Ops:
  0.6 70.1 %decoder_crps.1 = (bf16[2,1024,1024]{2,1,0:T(8,128)(2,1)S(1)}, f32[1024,1152]{1,0:T(8,128)S(1)}) custom-call(bf16[2,1024,1024]{2,1,0:T(8,128)(2,1)} %emb.1, bf16[1024,1024]{1,0:T(8,128)(2,1)} %w1_hbm.1, bf16[100,1024]{1,0:T(8,128)(2,1)} %bitcast.6, bf16[100,1024]{1,0:T(8,128)(2,1)} %target_hbm.1, f32[1,100]{1,0:T(1,128)} %bitcast.8, f32[8,128]{1,0:T(8,128)} %bitcast.7), custom_call_target="tpu_custom_call" | custom-call | flops 15000000512 | bytes 20000000 | tf_op jit(solution)/shard_map/decoder_crps/pallas_call | solution.py:476
  70.8 4.2 %write_out.1 = (bf16[2,1024,1024]{2,1,0:T(8,128)(2,1)}, f32[1024,1024]{1,0:T(8,128)}, f32[100,1024]{1,0:T(8,128)}, f32[1,1]{1,0:T(1,128)}) custom-call(bf16[2,1024,1024]{2,1,0:T(8,128)(2,1)S(1)} %get-tuple-element.10.ed, f32[1024,1152]{1,0:T(8,128)S(1)} %get-tuple-element.11.full), custom_call_target="tpu_custom_call" | custom-call | tf_op jit(solution)/shard_map/write_out/pallas_call | solution.py:530

commit v7 on v6

--- a/solution.py
+++ b/solution.py
@@ -321,15 +321,14 @@
 
     def to_core(u, s):
         at = (block_rows([along(u, 0, s)]), cols_of(u))
-        remote(full.at[at], full.at[at], cg_sem.at[NU], cg_sem.at[u], other_core).start()
+        remote(full.at[at], full.at[at], cg_sem.at[1], cg_sem.at[0], other_core).start()
 
     def ag1_receive(u):
         arrived(full.at[pl.ds(0, 96), cols_of(u)], ag1_sem.at[u])
         at = (block_rows([along(u, 0, 0)]), cols_of(u))
         for s in OFFSETS:
-            remote(
-                full.at[at], full.at[at], ag0_sem.at[NU], ag0_sem.at[u], peer_of(u, 0, s)
-            ).start()
+            sem = ag0_sem.at[u if u < NU - 3 else single(u, s)]
+            remote(full.at[at], full.at[at], ag0_sem.at[NU], sem, peer_of(u, 0, s)).start()
         to_core(u, 0)
 
     def ag0_receive(u):
@@ -337,8 +336,13 @@
         for s in OFFSETS:
             to_core(u, s)
 
-    def cg_receive(u):
-        arrived(full.at[pl.ds(0, HALF), cols_of(u)], cg_sem.at[u])
+    def single(u, s):
+        return NU + 1 + (u - (NU - 3)) * 3 + s - 1
+
+    def ag0_receive_block(u, s):
+        at = full.at[block_rows([along(u, 0, 4 - s)]), cols_of(u)]
+        arrived(at, ag0_sem.at[single(u, s)])
+        to_core(u, 4 - s)
 
     def run():
         load()
@@ -415,6 +419,7 @@
         embedding_derivative(1, 0)
         each(rs0_receive, 1)
         each(rs1_receive, 0)
+        embedding_derivative(0, 1)
         each(rs0_receive, 2)
         each(rs1_receive, 1)
         each(x_receive, 0)
@@ -422,15 +427,15 @@
         each(x_receive, 1)
         each(ag1_receive, 0)
         each(x_receive, 2)
+        embedding_derivative(1, 1)
         each(ag1_receive, 1)
         each(ag1_receive, 2)
-        embedding_derivative(0, 1)
         each(ag0_receive, 0)
-        embedding_derivative(1, 1)
         each(ag0_receive, 1)
-        each(ag0_receive, 2)
-        for wave in range(3):
-            each(cg_receive, wave)
+        for s in (1, 3, 2):
+            for u in waves[2]:
+                ag0_receive_block(u, s)
+        arrived(full.at[pl.ds(0, HALF)], cg_sem.at[0])
 
     run()
     left(av.at[pl.ds(0, 15)], area_sem.at[0])
@@ -442,7 +447,7 @@
     left(s3.at[:, pl.ds(0, 3)], x_sem.at[NU])
     left(s2, ag1_sem.at[NU])
     left(s1, ag0_sem.at[NU])
-    left(core_in, cg_sem.at[NU])
+    left(core_in, cg_sem.at[1])
 
 
 def finish(ed, full, ed_out, grad_out, grad_t_out, penalty, sem):
@@ -511,7 +516,7 @@
             dma((2,)),
             dma((NQ + 1,)), dma((NQ + 1,)),
             dma((NU + 1,)), dma((NU + 1,)), dma((NU + 1,)), dma((NU + 1,)),
-            dma((NU + 1,)), dma((NU + 1,)), dma((NU + 1,)),
+            dma((NU + 1,)), dma((NU + 10,)), dma((2,)),
         ],
         compiler_params=pltpu.CompilerParams(
             collective_id=0, has_side_effects=True, vmem_limit_bytes=50 * 2**20

time: 75.2 us -> 75.2 us (level)
  no operation moved by 1% of the time
where the time goes in v7:
time: 75.2 us; the launch traced here: 75.1 us
  Pallas kernels  74.3 us (99%)
  between operations  0.8 us (1%)
    pallas_call x1, Pallas kernels, per_device(): pl.pallas_call(kernel, name='decoder_crps', out_shape=in_vmem, in_specs=[...  70.1 us
    pallas_call x1, Pallas kernels, per_device(): pl.pallas_call(finish, name='write_out', out_shape=(jax.ShapeDtypeStruct(...  4.18 us

profile of v7, /device:TPU:1, one launch (start us, length us, event | category | flops | bytes accessed | tf_op | source)
XLA Modules:
  0.0 75.1 jit_solution(15035824514088495591)
XLA Ops:
  0.6 70.1 %decoder_crps.1 = (bf16[2,1024,1024]{2,1,0:T(8,128)(2,1)S(1)}, f32[1024,1152]{1,0:T(8,128)S(1)}) custom-call(bf16[2,1024,1024]{2,1,0:T(8,128)(2,1)} %emb.1, bf16[1024,1024]{1,0:T(8,128)(2,1)} %w1_hbm.1, bf16[100,1024]{1,0:T(8,128)(2,1)} %bitcast.6, bf16[100,1024]{1,0:T(8,128)(2,1)} %target_hbm.1, f32[1,100]{1,0:T(1,128)} %bitcast.8, f32[8,128]{1,0:T(8,128)} %bitcast.7), custom_call_target="tpu_custom_call" | custom-call | flops 15000000512 | bytes 20000000 | tf_op jit(solution)/shard_map/decoder_crps/pallas_call | solution.py:481
  70.8 4.2 %write_out.1 = (bf16[2,1024,1024]{2,1,0:T(8,128)(2,1)}, f32[1024,1024]{1,0:T(8,128)}, f32[100,1024]{1,0:T(8,128)}, f32[1,1]{1,0:T(1,128)}) custom-call(bf16[2,1024,1024]{2,1,0:T(8,128)(2,1)S(1)} %get-tuple-element.10.ed, f32[1024,1152]{1,0:T(8,128)S(1)} %get-tuple-element.11.full), custom_call_target="tpu_custom_call" | custom-call | tf_op jit(solution)/shard_map/write_out/pallas_call | solution.py:535

commit v8 on v7

--- a/solution.py
+++ b/solution.py
@@ -109,8 +109,7 @@
         for copy in small_copies:
             copy.start()
         w1_copy.start()
-        for q in range(NQ):
-            emb_copy(q).start()
+        emb_copy(0).start()
 
     def greet():
         peers = [(member_peer(o), g) for o in range(1, 8)]
@@ -181,8 +180,7 @@
     def pairwise(q):
         mine_r, mine_l = me // NL, me % NL
         lanes = ds(q * CQ + mine_l * 128, 128, 128)
-        mean = jnp.sum(jnp.sum(av[...], axis=0), keepdims=True) / TOTAL_CELLS
-        area = aw[pl.ds(q * NL + mine_l, 1), :] / mean
+        area = aw[pl.ds(q * NL + mine_l, 1), :]
 
         def tile(rows, n):
             scale = area * vcol[mine_r, rows, :]
@@ -349,6 +347,8 @@
         greet()
         small_operands()
         w1_copy.wait()
+        for q in range(1, NQ):
+            emb_copy(q).start()
         w1t[...] = w1[...].T
         forward(0, (0,))
         pl.semaphore_wait(barrier, 23)
@@ -361,6 +361,8 @@
         forward(2)
         send_all(2, fs, fr, f_sem)
         arrived(av.at[pl.ds(0, 15)], area_sem.at[1])
+        mean = jnp.sum(jnp.sum(av[...], axis=0), keepdims=True) / TOTAL_CELLS
+        aw[...] = aw[...] / mean
         receive_all(0, fr, f_sem)
         pairwise(0)
         send_all(0, gs, gr, g_sem)

time: 75.2 us -> 76.2 us (1.013)
  Pallas kernels: 74.3 us -> 75.3 us
    pallas_call x1, Pallas kernels: 70.1 us -> 71.1 us  [per_device(): pl.pallas_call(kernel, name='decoder_crps', out_shape=in_vmem, in_specs=[...]
where the time goes in v8:
time: 76.2 us; the launch traced here: 76.1 us
  Pallas kernels  75.3 us (99%)
  between operations  0.8 us (1%)
    pallas_call x1, Pallas kernels, per_device(): pl.pallas_call(kernel, name='decoder_crps', out_shape=in_vmem, in_specs=[...  71.1 us
    pallas_call x1, Pallas kernels, per_device(): pl.pallas_call(finish, name='write_out', out_shape=(jax.ShapeDtypeStruct(...  4.18 us

profile of v8, /device:TPU:1, one launch (start us, length us, event | category | flops | bytes accessed | tf_op | source)
XLA Modules:
  0.0 76.1 jit_solution(13389331029755177729)
XLA Ops:
  0.6 71.1 %decoder_crps.1 = (bf16[2,1024,1024]{2,1,0:T(8,128)(2,1)S(1)}, f32[1024,1152]{1,0:T(8,128)S(1)}) custom-call(bf16[2,1024,1024]{2,1,0:T(8,128)(2,1)} %emb.1, bf16[1024,1024]{1,0:T(8,128)(2,1)} %w1_hbm.1, bf16[100,1024]{1,0:T(8,128)(2,1)} %bitcast.6, bf16[100,1024]{1,0:T(8,128)(2,1)} %target_hbm.1, f32[1,100]{1,0:T(1,128)} %bitcast.8, f32[8,128]{1,0:T(8,128)} %bitcast.7), custom_call_target="tpu_custom_call" | custom-call | flops 15000000512 | bytes 20000000 | tf_op jit(solution)/shard_map/decoder_crps/pallas_call | solution.py:483
  71.8 4.2 %write_out.1 = (bf16[2,1024,1024]{2,1,0:T(8,128)(2,1)}, f32[1024,1024]{1,0:T(8,128)}, f32[100,1024]{1,0:T(8,128)}, f32[1,1]{1,0:T(1,128)}) custom-call(bf16[2,1024,1024]{2,1,0:T(8,128)(2,1)S(1)} %get-tuple-element.10.ed, f32[1024,1152]{1,0:T(8,128)S(1)} %get-tuple-element.11.full), custom_call_target="tpu_custom_call" | custom-call | tf_op jit(solution)/shard_map/write_out/pallas_call | solution.py:537
